TPU v7x, 32 devices: a whole 2x2x4 slice. The times are simulated.
32 devices in a mesh: dp: 8 (over z, x), seq: 4 (over y, core).
Axes of the slice: x: 2, y: 2, z: 4, core: 2. Of those that a mesh axis runs over, the one named last changes fastest.
Arguments:
- frames: bfloat16 [16, 4096, 256], P('dp', 'seq'), may hold values from -6 to 6
- time_embed: bfloat16 [16, 1024], P('dp'), may hold values from -6 to 6
- lengths: int32 [16], P('dp'), may hold values from 256 to 4096, as said below
- out_cotangent: bfloat16 [16, 2048, 256], P('dp', 'seq'), may hold values from -6 to 6
- conv_first: bfloat16 [3, 256, 256], replicated, may hold values from -0.21875 to 0.21875
- conv_second: bfloat16 [3, 256, 256], replicated, may hold values from -0.21875 to 0.21875
- conv_skip: bfloat16 [256, 256], replicated, may hold values from -0.375 to 0.375
- time_proj: bfloat16 [1024, 256], replicated, may hold values from -0.1875 to 0.1875
- w_qkv: bfloat16 [256, 384], replicated, may hold values from -0.375 to 0.375
- w_out: bfloat16 [128, 256], replicated, may hold values from -1.5 to 1.5
- ff_in: bfloat16 [256, 1024], replicated, may hold values from -0.375 to 0.375
- ff_out: bfloat16 [1024, 256], replicated, may hold values from -0.1875 to 0.1875
- conv_down: bfloat16 [3, 256, 256], replicated, may hold values from -0.21875 to 0.21875
- gains: float32 [4, 256], replicated, may hold values from 0.25 to 1.75
- shifts: float32 [11, 256], replicated, may hold values from -3 to 3
- ff_bias: float32 [1024], replicated, may hold values from -3 to 3
- snake_logs: float32 [2, 1024], replicated, may hold values from -0.7 to 0.7
Outputs:
- layer_out: bfloat16 [16, 2048, 256], P('dp', 'seq')
- grad_frames: float32 [16, 4096, 256], P('dp', 'seq')
- grad_conv_first: float32 [3, 256, 256], replicated
- grad_conv_second: float32 [3, 256, 256], replicated
- grad_conv_skip: float32 [256, 256], replicated
- grad_time_proj: float32 [1024, 256], replicated
- grad_w_qkv: float32 [256, 384], replicated
- grad_w_out: float32 [128, 256], replicated
- grad_ff_in: float32 [256, 1024], replicated
- grad_ff_out: float32 [1024, 256], replicated
- grad_conv_down: float32 [3, 256, 256], replicated
- grad_gains: float32 [4, 256], replicated
- grad_shifts: float32 [11, 256], replicated
- grad_ff_bias: float32 [1024], replicated
- grad_snake_logs: float32 [2, 1024], replicated
Inputs may be any that keep to these rules, and one draw needn't show every extreme that they name: `lengths`: each aligned block of 2 utterances holds one of full length 4096.
All inputs are finite; a program needn't handle non-finite values.
Results may differ from a plain program's by a relative error of at most 0.012.
The roundings to bfloat16 on the way count: a program that leaves them out, or rounds other values in their place, can miss the bound.
Values may be sent and summed in bfloat16 or wider, within the bound.
A program may use at most 320 MiB of HBM per device.

v0:
```python
import jax
import jax.numpy as jnp
from jax import lax
from jax.sharding import PartitionSpec as P

HEADS = 2
GROUPS = 8


norm_eps = 1e-05


def with_halo(x, sides, width):
    for axis, dim in sides:
        size, length = (lax.axis_size(axis), x.shape[dim])
        up = [(i, (i + 1) % size) for i in range(size - 1)]
        down = [(j, i) for i, j in up]
        last = lax.slice_in_dim(x, length - width, length, axis=dim)
        leading = lax.slice_in_dim(x, 0, width, axis=dim)
        before = lax.ppermute(last, axis, up)
        after = lax.ppermute(leading, axis, down)
        x = jnp.concatenate([before, x, after], axis=dim)
    return x


def from_behind(block, axis, distance):
    devices = range(lax.axis_size(axis))
    route = [(i - distance, i) for i in devices if i - distance in devices]
    return lax.ppermute(block, axis, route)


def mish(values):
    return values * jnp.tanh(jax.nn.softplus(values))


def project(operand, matrix):
    return lax.dot_general(
        operand, matrix, (((operand.ndim - 1,), (0,)), ((), ())), preferred_element_type=jnp.float32
    )


def project_back(grads, matrix):
    return lax.dot_general(
        grads, matrix, (((grads.ndim - 1,), (1,)), ((), ())), preferred_element_type=jnp.float32
    )


def weight_grad(operand, grads):
    flat_operand = operand.reshape(-1, operand.shape[-1])
    flat_grads = grads.reshape(-1, grads.shape[-1])
    return lax.dot_general(
        flat_operand, flat_grads, (((0,), (0,)), ((), ())), preferred_element_type=jnp.float32
    )


def conv_forward(values, weight):
    padded = with_halo(values, (("seq", 1),), 1)
    local_len = values.shape[1]
    stacked = jnp.concatenate(
        [padded[:, 0:local_len], padded[:, 1 : local_len + 1], padded[:, 2 : local_len + 2]], axis=2
    )
    return (stacked, project(stacked, weight.reshape(-1, weight.shape[2])))


def conv_backward(grads, weight):
    padded = with_halo(grads, (("seq", 1),), 1)
    local_len = grads.shape[1]
    stacked = jnp.concatenate(
        [padded[:, 2 : local_len + 2], padded[:, 1 : local_len + 1], padded[:, 0:local_len]], axis=2
    )
    flipped = jnp.transpose(weight, (0, 2, 1)).reshape(-1, weight.shape[1])
    return project(stacked, flipped)


def group_stats(hidden, frame_mask, counts):
    utt_count, frame_count, channels = hidden.shape
    grouped = hidden.reshape(utt_count, frame_count, GROUPS, channels // GROUPS)
    mask_cube = frame_mask[:, :, None, None]
    weighted = grouped * mask_cube
    group_mean = lax.psum(jnp.sum(weighted, axis=(1, 3)), "seq") / counts[:, None]
    centered = grouped - group_mean[:, None, :, None]
    variance = (
        lax.psum(jnp.sum(centered * centered * mask_cube, axis=(1, 3)), "seq") / counts[:, None]
    )
    return (group_mean, lax.rsqrt(variance + norm_eps))


def norm_mish(hidden, group_mean, inv_std, gain, shift, frame_mask):
    utt_count, frame_count, channels = hidden.shape
    grouped = hidden.reshape(utt_count, frame_count, GROUPS, channels // GROUPS)
    normed = ((grouped - group_mean[:, None, :, None]) * inv_std[:, None, :, None]).reshape(
        hidden.shape
    )
    return mish(normed * gain + shift) * frame_mask[:, :, None]


def norm_backward(grads, hidden, group_mean, inv_std, gain, shift, frame_mask, counts):

    def local_piece(hidden_v, mean_v, inv_v, gain_v, shift_v):
        return norm_mish(hidden_v, mean_v, inv_v, gain_v, shift_v, frame_mask)

    outputs, pullback = jax.vjp(local_piece, hidden, group_mean, inv_std, gain, shift)
    grad_hidden, grad_mean, grad_inv, grad_gain, grad_shift = pullback(grads)
    grad_mean, grad_inv = lax.psum((grad_mean, grad_inv), "seq")
    grad_variance = grad_inv * -0.5 * inv_std * inv_std * inv_std
    utt_count, frame_count, channels = hidden.shape
    grouped = hidden.reshape(utt_count, frame_count, GROUPS, channels // GROUPS)
    extra_grad = (
        grad_mean[:, None, :, None]
        + 2.0 * grad_variance[:, None, :, None] * (grouped - group_mean[:, None, :, None])
    ) / counts[:, None, None, None]
    grad_hidden = grad_hidden + (extra_grad * frame_mask[:, :, None, None]).reshape(hidden.shape)
    return (grad_hidden, grad_gain, grad_shift)


def layer_norm(values, gain, shift):
    centered = values - jnp.mean(values, axis=-1, keepdims=True)
    variance = jnp.mean(centered * centered, axis=-1, keepdims=True)
    return centered * lax.rsqrt(variance + norm_eps) * gain + shift


def snake(values, snake_logs):
    return values + jnp.square(jnp.sin(values * jnp.exp(snake_logs[0]))) / (
        jnp.exp(snake_logs[1]) + 1e-09
    )


def shards(
    frames,
    time_embed,
    lengths,
    out_cotangent,
    conv_first,
    conv_second,
    conv_skip,
    time_proj,
    w_qkv,
    w_out,
    ff_in,
    ff_out,
    conv_down,
    gains,
    shifts,
    ff_bias,
    snake_logs,
):
    utt_count, frame_count, channels = frames.shape
    whole_len = frame_count * lax.axis_size("seq")
    inner_width = w_out.shape[0]
    head_dim = inner_width // HEADS
    score_scale = head_dim ** (-0.5)
    positions = lax.axis_index("seq") * frame_count + jnp.arange(frame_count)
    frame_mask = (positions[None, :] < lengths[:, None]).astype(jnp.float32)
    key_mask = jnp.arange(whole_len)[None, :] < lengths[:, None]
    counts = lengths.astype(jnp.float32) * (channels // GROUPS)
    column_mask = frame_mask[:, :, None]
    masked_in = frames * column_mask.astype(jnp.bfloat16)
    taps_one, product_one = conv_forward(masked_in, conv_first)
    hidden_one = product_one + shifts[0]
    mean_one, inv_one = group_stats(hidden_one, frame_mask, counts)
    act_one = norm_mish(hidden_one, mean_one, inv_one, gains[0], shifts[1], frame_mask)
    embed_act = mish(time_embed.astype(jnp.float32)).astype(jnp.bfloat16)
    time_shift = jnp.dot(embed_act, time_proj, preferred_element_type=jnp.float32) + shifts[2]
    act_in = ((act_one + time_shift[:, None, :]) * column_mask).astype(jnp.bfloat16)
    taps_two, product_two = conv_forward(act_in, conv_second)
    hidden_two = product_two + shifts[3]
    mean_two, inv_two = group_stats(hidden_two, frame_mask, counts)
    act_two = norm_mish(hidden_two, mean_two, inv_two, gains[1], shifts[4], frame_mask)
    resnet_out = act_two + project(masked_in, conv_skip) + shifts[5]
    normed_one = layer_norm(resnet_out, gains[2], shifts[6]).astype(jnp.bfloat16)
    qkv_rows = project(normed_one, w_qkv).astype(jnp.bfloat16)
    queries = qkv_rows[:, :, :inner_width].reshape(utt_count, frame_count, HEADS, head_dim)
    keys_all, values_all = (
        lax.all_gather(qkv_rows[:, :, inner_width : 2 * inner_width], "seq", axis=1, tiled=True),
        lax.all_gather(qkv_rows[:, :, 2 * inner_width :], "seq", axis=1, tiled=True),
    )
    keys_all = keys_all.reshape(utt_count, whole_len, HEADS, head_dim)
    values_all = values_all.reshape(utt_count, whole_len, HEADS, head_dim)

    def attention_scores():
        raw_scores = jnp.einsum(
            "uqhd,ukhd->uhqk", queries, keys_all, preferred_element_type=jnp.float32
        )
        return jnp.where(key_mask[:, None, None, :], raw_scores * score_scale, -1000000000.0)

    scores = attention_scores()
    row_top = jnp.max(scores, axis=-1, keepdims=True)
    log_total = row_top + jnp.log(jnp.sum(jnp.exp(scores - row_top), axis=-1, keepdims=True))
    probs_low = jnp.exp(scores - log_total).astype(jnp.bfloat16)
    attended = jnp.einsum(
        "uhqk,ukhd->uqhd", probs_low, values_all, preferred_element_type=jnp.float32
    )
    attended = attended.astype(jnp.bfloat16).reshape(utt_count, frame_count, inner_width)
    resid_two = resnet_out + project(attended, w_out) + shifts[7]
    normed_two = layer_norm(resid_two, gains[3], shifts[8]).astype(jnp.bfloat16)
    ff_hidden = project(normed_two, ff_in) + ff_bias
    snaked = snake(ff_hidden, snake_logs).astype(jnp.bfloat16)
    resid_three = resid_two + project(snaked, ff_out) + shifts[9]
    down_in = (resid_three * column_mask).astype(jnp.bfloat16)
    half_len = frame_count // 2
    before_first = from_behind(down_in[:, frame_count - 1 :], "seq", 1)
    frame_pairs = down_in.reshape(utt_count, half_len, 2, channels)
    even_rows = frame_pairs[:, :, 0]
    odd_rows = frame_pairs[:, :, 1]
    before = jnp.concatenate([before_first, odd_rows[:, : half_len - 1]], axis=1)
    taps_down = jnp.concatenate([before, even_rows, odd_rows], axis=2)
    half_mask = frame_mask[:, 0::2][:, :, None]
    lowered = project(taps_down, conv_down.reshape(-1, channels)) + shifts[10]
    layer_out = (lowered * half_mask).astype(jnp.bfloat16)
    grad_lowered = out_cotangent.astype(jnp.float32) * half_mask
    grad_shift_down = jnp.sum(grad_lowered, axis=(0, 1))
    grad_low = grad_lowered.astype(jnp.bfloat16)
    grad_conv_down = weight_grad(taps_down, grad_low).reshape(3, channels, channels)
    grad_taps = project_back(grad_low, conv_down.reshape(-1, channels))
    grad_before = grad_taps[:, :, :channels]
    grad_evens = grad_taps[:, :, channels : 2 * channels]
    grad_odds = grad_taps[:, :, 2 * channels :]
    from_next = from_behind(grad_before[:, 0:1], "seq", -1)
    grad_odds = grad_odds + jnp.concatenate([grad_before[:, 1:], from_next], axis=1)
    grad_down_in = jnp.stack([grad_evens, grad_odds], axis=2).reshape(
        utt_count, frame_count, channels
    )
    grad_three = grad_down_in * column_mask
    grad_shift_ff = jnp.sum(grad_three, axis=(0, 1))
    grad_ff_low = grad_three.astype(jnp.bfloat16)
    grad_ff_out = weight_grad(snaked, grad_ff_low)
    grad_snaked = project_back(grad_ff_low, ff_out)
    outputs, snake_pull = jax.vjp(snake, ff_hidden, snake_logs)
    grad_hidden, grad_snake_logs = snake_pull(grad_snaked)
    grad_ff_bias = jnp.sum(grad_hidden, axis=(0, 1))
    grad_hidden_low = grad_hidden.astype(jnp.bfloat16)
    grad_ff_in = weight_grad(normed_two, grad_hidden_low)
    grad_normed_two = project_back(grad_hidden_low, ff_in)
    outputs, norm_pull_two = jax.vjp(layer_norm, resid_two, gains[3], shifts[8])
    grad_resid_norm, grad_gain_three, grad_shift_three = norm_pull_two(grad_normed_two)
    grad_two = grad_three + grad_resid_norm
    grad_shift_attn = jnp.sum(grad_two, axis=(0, 1))
    grad_attn_low = grad_two.astype(jnp.bfloat16)
    grad_w_out = weight_grad(attended, grad_attn_low)
    grad_attended = project_back(grad_attn_low, w_out).astype(jnp.bfloat16)
    grad_attended = grad_attended.reshape(utt_count, frame_count, HEADS, head_dim)
    probs_full = jnp.exp(attention_scores() - log_total)
    probs_again = probs_full.astype(jnp.bfloat16)
    grad_probs = jnp.einsum(
        "uqhd,ukhd->uhqk", grad_attended, values_all, preferred_element_type=jnp.float32
    )
    row_terms = jnp.sum(probs_full * grad_probs, axis=-1, keepdims=True)
    grad_scores = (probs_full * (grad_probs - row_terms) * score_scale).astype(jnp.bfloat16)
    grad_queries = jnp.einsum(
        "uhqk,ukhd->uqhd", grad_scores, keys_all, preferred_element_type=jnp.float32
    )
    key_terms = jnp.einsum(
        "uhqk,uqhd->ukhd", grad_scores, queries, preferred_element_type=jnp.float32
    )
    value_terms = jnp.einsum(
        "uhqk,uqhd->ukhd", probs_again, grad_attended, preferred_element_type=jnp.float32
    )
    grad_keys, grad_values = (
        lax.psum_scatter(
            key_terms.reshape(utt_count, whole_len, inner_width).astype(jnp.bfloat16),
            "seq",
            scatter_dimension=1,
            tiled=True,
        ).astype(jnp.float32),
        lax.psum_scatter(
            value_terms.reshape(utt_count, whole_len, inner_width).astype(jnp.bfloat16),
            "seq",
            scatter_dimension=1,
            tiled=True,
        ).astype(jnp.float32),
    )
    grad_qkv = jnp.concatenate(
        [grad_queries.reshape(utt_count, frame_count, inner_width), grad_keys, grad_values], axis=2
    ).astype(jnp.bfloat16)
    grad_w_qkv = weight_grad(normed_one, grad_qkv)
    grad_normed_one = project_back(grad_qkv, w_qkv)
    outputs, norm_pull_one = jax.vjp(layer_norm, resnet_out, gains[2], shifts[6])
    grad_resid_one, grad_gain_two, grad_shift_two = norm_pull_one(grad_normed_one)
    grad_one = grad_two + grad_resid_one
    upper_gains = jnp.stack([grad_gain_two, grad_gain_three])
    upper_shifts = jnp.stack(
        [grad_shift_two, grad_shift_attn, grad_shift_three, grad_shift_ff, grad_shift_down]
    )
    upper_sums = (
        grad_conv_down,
        grad_w_qkv,
        grad_w_out,
        grad_ff_in,
        grad_ff_out,
        grad_ff_bias,
        grad_snake_logs,
        upper_gains,
        upper_shifts,
    )
    grad_shift_skip = jnp.sum(grad_one, axis=(0, 1))
    grad_skip_low = grad_one.astype(jnp.bfloat16)
    grad_conv_skip = weight_grad(masked_in, grad_skip_low)
    grad_masked = project_back(grad_skip_low, conv_skip)
    grad_hidden_two, grad_gain_norm_two, grad_shift_norm_two = norm_backward(
        grad_one, hidden_two, mean_two, inv_two, gains[1], shifts[4], frame_mask, counts
    )
    grad_shift_conv_two = jnp.sum(grad_hidden_two, axis=(0, 1))
    grad_two_low = grad_hidden_two.astype(jnp.bfloat16)
    grad_conv_second = weight_grad(taps_two, grad_two_low).reshape(3, channels, channels)
    grad_act_in = conv_backward(grad_two_low, conv_second) * column_mask
    grad_time = jnp.sum(grad_act_in, axis=1)
    grad_shift_time = jnp.sum(grad_time, axis=0)
    grad_time_proj = jnp.sum(
        embed_act.astype(jnp.float32)[:, :, None] * grad_time[:, None, :], axis=0
    )
    grad_hidden_one, grad_gain_norm_one, grad_shift_norm_one = norm_backward(
        grad_act_in, hidden_one, mean_one, inv_one, gains[0], shifts[1], frame_mask, counts
    )
    grad_shift_conv_one = jnp.sum(grad_hidden_one, axis=(0, 1))
    grad_one_low = grad_hidden_one.astype(jnp.bfloat16)
    grad_conv_first = weight_grad(taps_one, grad_one_low).reshape(3, channels, channels)
    grad_masked = grad_masked + conv_backward(grad_one_low, conv_first)
    grad_frames = grad_masked * column_mask
    lower_gains = jnp.stack([grad_gain_norm_one, grad_gain_norm_two])
    lower_shifts = jnp.stack(
        [
            grad_shift_conv_one,
            grad_shift_norm_one,
            grad_shift_time,
            grad_shift_conv_two,
            grad_shift_norm_two,
            grad_shift_skip,
        ]
    )
    summed = lax.psum(
        (
            grad_conv_first,
            grad_conv_second,
            grad_conv_skip,
            grad_time_proj,
            lower_gains,
            lower_shifts,
            upper_sums[0],
            upper_sums[1],
            upper_sums[2],
            upper_sums[3],
            upper_sums[4],
            upper_sums[5],
            upper_sums[6],
            upper_sums[7],
            upper_sums[8],
        ),
        ("dp", "seq"),
    )
    lower_sums = summed[:6]
    upper_sums = summed[6:]
    grad_gains = jnp.concatenate([lower_sums[4], upper_sums[7]], axis=0)
    grad_shifts = jnp.concatenate([lower_sums[5], upper_sums[8]], axis=0)
    return (
        layer_out,
        grad_frames,
        lower_sums[0],
        lower_sums[1],
        lower_sums[2],
        lower_sums[3],
        upper_sums[1],
        upper_sums[2],
        upper_sums[3],
        upper_sums[4],
        upper_sums[0],
        grad_gains,
        grad_shifts,
        upper_sums[5],
        upper_sums[6],
    )


def solution(mesh):
    in_specs = (
        P("dp", "seq", None),
        P("dp", None),
        P("dp"),
        P("dp", "seq", None),
        P(),
        P(),
        P(),
        P(),
        P(),
        P(),
        P(),
        P(),
        P(),
        P(),
        P(),
        P(),
        P(),
    )
    out_specs = (
        P("dp", "seq", None),
        P("dp", "seq", None),
        P(),
        P(),
        P(),
        P(),
        P(),
        P(),
        P(),
        P(),
        P(),
        P(),
        P(),
        P(),
        P(),
    )
    return jax.shard_map(shards, mesh=mesh, in_specs=in_specs, out_specs=out_specs, check_vma=False)
```

profile of v0, /device:TPU:1, one launch (start us, length us, event | category | flops | bytes accessed | tf_op | source)
XLA Modules:
  0.0 756.6 jit_solution(16045285042062677882)
XLA Ops:
  9.7 4.5 collective-permute-start
  22.0 5.1 psum.161
  27.9 6.0 psum.162
  36.5 3.9 collective-permute-start.2
  48.2 5.2 psum.163
  54.2 6.0 psum.164
  61.1 3.4 fusion.160
  81.2 11.8 %all-gather.5.cloned.1.call-done = bf16[2,4096,128]{1,2,0:T(8,128)(2,1)} async-done(((bf16[2,1024,128]{1,2,0:T(8,128)(2,1)}), bf16[2,4096,128]{1,2,0:T(8,128)(2,1)}) %all-gather.5.cloned.1.call-update) | async-done | bytes 2097168 | tf_op jit(solution)/shard_map/all_gather | solution.py:174
  93.0 25.8 %fusion.3 = (f32[2,2,1024]{2,1,0:T(2,128)S(1)}, f32[2,2,1024,4096]{3,2,1,0:T(8,128)}) fusion(pred[2,4096]{1,0:T(4,128)(4,1)S(1)} %iota_compare_fusion, bf16[2,1024,2,64]{1,3,2,0:T(8,128)(2,1)S(1)} %bitcast.197, bf16[2,4096,2,64]{1,3,2,0:T(8,128)(2,1)} %bitcast.199), kind=kOutput, calls=%fused_computation.8 | convolution fusion | flops 2197811200 | bytes 69754880 | tf_op jit(solution)/shard_map/uqhd,ukhd->uhqk/dot_general | solution.py:181
  118.9 21.4 %exponential_reduce_fusion = f32[2,2,1024]{2,1,0:T(2,128)S(1)} fusion(f32[2,2,1024,4096]{3,2,1,0:T(8,128)} %get-tuple-element.123, f32[2,2,1024]{2,1,0:T(2,128)S(1)} %get-tuple-element.122, pred[2,4096]{1,0:T(4,128)(4,1)S(1)} %iota_compare_fusion), kind=kLoop, calls=%fused_computation.6 | loop fusion | flops 67104768 | bytes 67149824 | tf_op jit(solution)/shard_map/reduce_sum | solution.py:188
  140.4 24.6 %convolution_convert_fusion.3 = bf16[2,2,64,1024]{3,2,1,0:T(8,128)(2,1)S(1)} fusion(bf16[2,4096,2,64]{1,3,2,0:T(8,128)(2,1)} %bitcast.201, f32[2,2,1024,4096]{3,2,1,0:T(8,128)} %get-tuple-element.123, f32[2,2,1024]{2,1,0:T(2,128)S(1)} %log_add_fusion, pred[2,4096]{1,0:T(4,128)(4,1)S(1)} %iota_compare_fusion), kind=kOutput, calls=%fused_computation.135 | convolution fusion | flops 2214854656 | bytes 69754880 | tf_op jit(solution)/shard_map/uhqk,ukhd->uqhd/dot_general | solution.py:190
  170.0 38.6 %multiply_reduce_fusion.2 = (f32[1024]{0:T(1024)}, f32[1024]{0:T(1024)}, f32[1024]{0:T(1024)}, bf16[2,1024,1024]{2,1,0:T(8,128)(2,1)S(1)}, bf16[2,1024,1024]{2,1,0:T(8,128)(2,1)}) fusion(f32[2,1024,1024]{2,1,0:T(8,128)S(1)} %fusion.96, f32[1024]{0:T(1024)S(1)} %multiply_divide_fusion, f32[1024]{0:T(1024)S(1)} %bitcast.269, f32[1024]{0:T(1024)S(1)} %copy-done.122, ...), kind=kOutput, calls=%fused_computation.17 | convolution fusion | flops 1114633216 | bytes 19435520 | tf_op jit(solution)/shard_map/dot_general | solution.py:43
  216.8 25.6 %convolution_convert_fusion = bf16[2,2,64,4096]{3,2,1,0:T(8,128)(2,1)} fusion(bf16[2,1024,2,64]{1,3,2,0:T(8,128)(2,1)S(1)} %bitcast.195, f32[2,2,1024,4096]{3,2,1,0:T(8,128)} %get-tuple-element.123, f32[2,2,1024]{2,1,0:T(2,128)S(1)} %log_add_fusion, pred[2,4096]{1,0:T(4,128)(4,1)S(1)} %iota_compare_fusion), kind=kOutput, calls=%fused_computation.29 | convolution fusion | flops 2215641088 | bytes 69754880 | tf_op jit(solution)/shard_map/uhqk,uqhd->ukhd/dot_general | solution.py:255
  242.4 4.1 copy.71
  246.5 26.3 %fusion.163 = f32[2,2,1024,4096]{3,2,1,0:T(8,128)} fusion(bf16[2,1024,2,64]{1,3,2,0:T(8,128)(2,1)S(1)} %bitcast.196, bf16[2,4096,2,64]{1,3,2,0:T(8,128)(2,1)} %bitcast.202), kind=kOutput, calls=%fused_computation.247 | convolution fusion | flops 2147483648 | bytes 69730304 | tf_op jit(solution)/shard_map/uqhd,ukhd->uhqk/dot_general | solution.py:244
  272.9 103.9 %fusion.17 = bf16[2,2,64,4096]{3,2,1,0:T(8,128)(2,1)} fusion(bf16[2,1024,2,64]{1,3,2,0:T(8,128)(2,1)} %bitcast.198, f32[2,2,1024,4096]{3,2,1,0:T(8,128)} %fusion.163, f32[2,2,1024,4096]{3,2,1,0:T(8,128)} %get-tuple-element.123, f32[2,2,1024]{2,1,0:T(2,128)S(1)} %log_add_fusion, pred[2,4096]{1,0:T(4,128)(4,1)S(1)} %iota_compare_fusion), kind=kOutput, calls=%fused_computation.28 | convolution fusion | flops 2333089792 | bytes 136863744 | tf_op jit(solution)/shard_map/uhqk,uqhd->ukhd/dot_general | solution.py:252
  376.8 4.1 copy.70
  382.8 4.7 copy.75
  387.6 4.9 copy.76
  392.5 3.4 multiply_convert_fusion.1
  404.8 5.1 convolution_bitcast_fusion
  412.7 102.2 %fusion.82 = bf16[2,2,64,1024]{3,2,1,0:T(8,128)(2,1)S(1)} fusion(bf16[2,4096,2,64]{1,3,2,0:T(8,128)(2,1)} %bitcast.200, f32[2,2,1024,4096]{3,2,1,0:T(8,128)} %fusion.163, f32[2,2,1024,4096]{3,2,1,0:T(8,128)} %get-tuple-element.123, f32[2,2,1024]{2,1,0:T(2,128)S(1)} %log_add_fusion, pred[2,4096]{1,0:T(4,128)(4,1)S(1)} %iota_compare_fusion), kind=kOutput, calls=%fused_computation.134 | convolution fusion | flops 2332303360 | bytes 136863744 | tf_op jit(solution)/shard_map/uhqk,ukhd->uqhd/dot_general | solution.py:249
  529.8 5.0 multiply_reduce_fusion.6
  535.2 5.3 all-reduce.5
  540.9 3.7 fusion.147
  547.3 3.2 collective-permute-start.7
  556.5 6.5 multiply_reduce_fusion.7
  563.3 5.1 all-reduce.4
  568.8 3.1 fusion.148
  590.9 41.1 %all-reduce.2 = (f32[2,256]{1,0:T(2,128)S(1)}, f32[2,256]{1,0:T(2,128)S(1)}, f32[5,256]{1,0:T(8,128)S(1)}, f32[6,256]{1,0:T(8,128)S(1)}, f32[1024]{0:T(1024)}, /*index=5*/f32[2,1024]{1,0:T(2,128)}) all-reduce(f32[2,256]{1,0:T(2,128)S(1)} %get-tuple-element.130, ...), channel_id=1, replica_groups=mesh['dp'=8,'seq'=4] {'dp','seq'}, use_global_device_ids=true, to_apply=%region_53.55 | all-reduce | flops 6912 | bytes 55296 | tf_op jit(solution)/shard_map/psum | solution.py:330
  633.2 4.9 add_multiply_fusion
  638.2 101.3 %all-reduce.8.cloned.1.call-done = (f32[3,256,256]{2,1,0:T(8,128)}, f32[3,256,256]{2,1,0:T(8,128)}, f32[256,256]{1,0:T(8,128)}, f32[1024,256]{1,0:T(8,128)}, f32...) async-done(((f32[3,256,256]{2,1,0:T(8,128)}, f32[3,256,256]{2,1,0:T(8,128)}, ...) | async-done | bytes 6291472 | tf_op jit(solution)/shard_map/psum | solution.py:330
  (414 shorter events, 120.8 us)
Async XLA Ops:
  7.2 162.6 %copy-start = (bf16[1024,256]{1,0:T(8,128)(2,1)S(1)}, bf16[1024,256]{1,0:T(8,128)(2,1)}, u32[]{:S(2)}) copy-start(bf16[1024,256]{1,0:T(8,128)(2,1)} %param.29) | copy-start | bytes 1572868
  7.2 85.8 %all-gather.5.cloned.1.call-start = ((), (), s32[]{:S(2)}) async-start(), calls=%async_computation.3 | async-start | bytes 2621440 | tf_op jit(solution)/shard_map/all_gather | solution.py:174
  9.7 7.4 collective-permute-start
  14.3 4.9 collective-permute-start.1
  16.3 18.3 %copy-start.92 = (f32[1,256]{1,0:T(1,128)}, f32[1,256]{1,0:T(1,128)S(1)}, u32[]{:S(2)}) copy-start(f32[1,256]{1,0:T(1,128)S(1)} %get-tuple-element.114) | copy-start | bytes 3076
  16.3 44.8 %copy-start.94 = (f32[1,256]{1,0:T(1,128)}, f32[1,256]{1,0:T(1,128)S(1)}, u32[]{:S(2)}) copy-start(f32[1,256]{1,0:T(1,128)S(1)} %get-tuple-element.113) | copy-start | bytes 3076
  16.3 49.0 %copy-start.86 = (f32[1,256]{1,0:T(1,128)}, f32[1,256]{1,0:T(1,128)S(1)}, u32[]{:S(2)}) copy-start(f32[1,256]{1,0:T(1,128)S(1)} %get-tuple-element.115) | copy-start | bytes 3076
  16.9 17.7 %copy-start.82 = (f32[1,256]{1,0:T(1,128)}, f32[1,256]{1,0:T(1,128)S(1)}, u32[]{:S(2)}) copy-start(f32[1,256]{1,0:T(1,128)S(1)} %get-tuple-element.104) | copy-start | bytes 3076
  16.9 17.7 %copy-start.100 = (f32[1,256]{1,0:T(1,128)}, f32[1,256]{1,0:T(1,128)S(1)}, u32[]{:S(2)}) copy-start(f32[1,256]{1,0:T(1,128)S(1)} %get-tuple-element.103) | copy-start | bytes 3076
  16.9 44.2 %copy-start.84 = (f32[1,256]{1,0:T(1,128)}, f32[1,256]{1,0:T(1,128)S(1)}, u32[]{:S(2)}) copy-start(f32[1,256]{1,0:T(1,128)S(1)} %get-tuple-element.101) | copy-start | bytes 3076
  16.9 44.2 %copy-start.104 = (f32[1,256]{1,0:T(1,128)}, f32[1,256]{1,0:T(1,128)S(1)}, u32[]{:S(2)}) copy-start(f32[1,256]{1,0:T(1,128)S(1)} %get-tuple-element.100) | copy-start | bytes 3076
  16.9 48.4 %copy-start.102 = (f32[1,256]{1,0:T(1,128)}, f32[1,256]{1,0:T(1,128)S(1)}, u32[]{:S(2)}) copy-start(f32[1,256]{1,0:T(1,128)S(1)} %get-tuple-element.98) | copy-start | bytes 3076
  16.9 151.2 %copy-start.73 = (f32[1,256]{1,0:T(1,128)}, f32[1,256]{1,0:T(1,128)S(1)}, u32[]{:S(2)}) copy-start(f32[1,256]{1,0:T(1,128)S(1)} %get-tuple-element.96) | copy-start | bytes 3076
  17.1 43.1 %copy-start.65 = (f32[2]{0:T(128)}, f32[2]{0:T(128)S(1)}, u32[]{:S(2)}) copy-start(f32[2]{0:T(128)S(1)} %convert_multiply_fusion.2) | copy-start | bytes 28
  21.8 14.7 %copy-start.8 = (f32[2,1024,256]{2,1,0:T(8,128)}, f32[2,1024,256]{2,1,0:T(8,128)S(1)}, u32[]{:S(2)}) copy-start(f32[2,1024,256]{2,1,0:T(8,128)S(1)} %get-tuple-element.117) | copy-start | bytes 6291460
  36.5 6.0 collective-permute-start.2
  40.4 5.0 collective-permute-start.3
  48.0 16.5 %copy-start.6 = (f32[2,1024,256]{2,1,0:T(8,128)}, f32[2,1024,256]{2,1,0:T(8,128)S(1)}, u32[]{:S(2)}) copy-start(f32[2,1024,256]{2,1,0:T(8,128)S(1)} %get-tuple-element.119) | copy-start | bytes 6291460
  48.0 13.1 %copy-start.61 = (bf16[256,256]{1,0:T(8,128)(2,1)S(1)}, bf16[256,256]{1,0:T(8,128)(2,1)}, u32[]{:S(2)}) copy-start(bf16[256,256]{1,0:T(8,128)(2,1)} %param.24) | copy-start | bytes 393220
  68.4 24.6 %copy-start.30 = (bf16[2,1024,128]{1,2,0:T(8,128)(2,1)}, bf16[2,1024,128]{1,2,0:T(8,128)(2,1)S(1)}, u32[]{:S(2)}) copy-start(bf16[2,1024,128]{1,2,0:T(8,128)(2,1)S(1)} %get-tuple-element.81) | copy-start | bytes 1572868
  68.4 71.9 %all-gather.3.cloned.1.call-start = ((), (), s32[]{:S(2)}) async-start(), calls=%async_computation.2 | async-start | bytes 2621440 | tf_op jit(solution)/shard_map/all_gather | solution.py:175
  70.7 5.2 collective-permute-start.5
  81.2 441.7 %reduce-scatter.5.cloned.1.call-start = ((), (), s32[]{:S(2)}) async-start(), calls=%async_computation.5 | async-start | bytes 2621440 | tf_op jit(solution)/shard_map/reduce_scatter | solution.py:265
  140.3 24.6 %copy-start.53 = (bf16[128,256]{1,0:T(8,128)(2,1)S(1)}, bf16[128,256]{1,0:T(8,128)(2,1)}, u32[]{:S(2)}) copy-start(bf16[128,256]{1,0:T(8,128)(2,1)} %param.27) | copy-start | bytes 196612
  246.5 276.4 %reduce-scatter.3.cloned.1.call-start = ((), (), s32[]{:S(2)}) async-start(), calls=%async_computation.4 | async-start | bytes 2621440 | tf_op jit(solution)/shard_map/reduce_scatter | solution.py:259
  380.9 358.5 %all-reduce.8.cloned.1.call-start = ((), (), s32[]{:S(2)}) async-start(), calls=%async_computation.6 | async-start | bytes 12582912 | tf_op jit(solution)/shard_map/psum | solution.py:330
  399.9 117.7 %collective-permute-start.4 = (bf16[2,1,256]{2,1,0:T(2,128)(2,1)S(1)}, bf16[2,1,256]{2,1,0:T(2,128)(2,1)S(1)}, u32[]{:S(2)}, u32[]{:S(2)}) collective-permute-start(bf16[2,1,256]{2,1,0:T(2,128)(2,1)S(1)} %slice.206), channel_id=1, source_target_pairs={{0,1},{1,2},{2,3},{4,5},{5,6},{6,7},{8,9},{9,10},{10,11},{12,13},{... | collective-permute-start | bytes 3080 | tf_op jit(solution)/shard_map/ppermute | solution.py:29
  412.7 102.2 %copy-start.17 = (bf16[2,1024,256]{2,1,0:T(8,128)(2,1)S(1)}, bf16[2,1024,256]{2,1,0:T(8,128)(2,1)}, u32[]{:S(2)}) copy-start(bf16[2,1024,256]{2,1,0:T(8,128)(2,1)} %copy-done.16) | copy-start | bytes 3145732
  544.6 11.4 %collective-permute-start.6 = (bf16[2,1,256]{2,1,0:T(2,128)(2,1)S(1)}, bf16[2,1,256]{2,1,0:T(2,128)(2,1)S(1)}, u32[]{:S(2)}, u32[]{:S(2)}) collective-permute-start(bf16[2,1,256]{2,1,0:T(2,128)(2,1)S(1)} %get-tuple-element.85), channel_id=1, source_target_pairs={{1,0},{2,1},{3,2},{5,4},{6,5},{7,6},{9,8},{10,9},{11,10},{13,12},{... | collective-permute-start | bytes 3080 | tf_op jit(solution)/shard_map/ppermute | solution.py:21
  547.3 8.7 %collective-permute-start.7 = (bf16[2,1,256]{2,1,0:T(2,128)(2,1)S(1)}, bf16[2,1,256]{2,1,0:T(2,128)(2,1)S(1)}, u32[]{:S(2)}, u32[]{:S(2)}) collective-permute-start(bf16[2,1,256]{2,1,0:T(2,128)(2,1)S(1)} %get-tuple-element.86), channel_id=1, source_target_pairs={{0,1},{1,2},{2,3},{4,5},{5,6},{6,7},{8,9},{9,10},{10,11},{12,13},{... | collective-permute-start | bytes 3080 | tf_op jit(solution)/shard_map/ppermute | solution.py:20
  584.6 48.6 %collective-permute-start.8 = (bf16[2,1,256]{2,1,0:T(2,128)(2,1)S(1)}, bf16[2,1,256]{2,1,0:T(2,128)(2,1)S(1)}, u32[]{:S(2)}, u32[]{:S(2)}) collective-permute-start(bf16[2,1,256]{2,1,0:T(2,128)(2,1)S(1)} %get-tuple-element.83), channel_id=1, source_target_pairs={{1,0},{2,1},{3,2},{5,4},{6,5},{7,6},{9,8},{10,9},{11,10},{13,12},{... | collective-permute-start | bytes 3080 | tf_op jit(solution)/shard_map/ppermute | solution.py:21
  587.6 45.6 %collective-permute-start.9 = (bf16[2,1,256]{2,1,0:T(2,128)(2,1)S(1)}, bf16[2,1,256]{2,1,0:T(2,128)(2,1)S(1)}, u32[]{:S(2)}, u32[]{:S(2)}) collective-permute-start(bf16[2,1,256]{2,1,0:T(2,128)(2,1)S(1)} %get-tuple-element.84), channel_id=1, source_target_pairs={{0,1},{1,2},{2,3},{4,5},{5,6},{6,7},{8,9},{9,10},{10,11},{12,13},{... | collective-permute-start | bytes 3080 | tf_op jit(solution)/shard_map/ppermute | solution.py:20
  (106 other events, 423.9 us)
Sparse Core Ops, SparseCore 0:
  68.6 24.4 all-gather.4
  95.1 22.5 all-gather.2
  246.6 31.0 reduce-scatter.4
  381.0 31.0 reduce-scatter.2
  575.8 163.6 all-reduce.7
where the time goes:
time: 766 us; the launch traced here: 757 us
  matrix products  403 us (53%)
  waiting for transfers between devices  120 us (16%)
  blocking collectives  74 us (10%)
  local copies, waits for them, and re-layouts  57.8 us (8%)
  other arithmetic  56.2 us (7%)
  starting transfers between devices  29.5 us (4%)
  between operations  15.7 us (2%)
    dot_general x1, matrix products, shards(): jnp.einsum('uhqk,uqhd->ukhd', grad_scores, queries, preferred_element_typ...  104 us
    dot_general x1, matrix products, shards(): jnp.einsum('uhqk,ukhd->uqhd', grad_scores, keys_all, preferred_element_ty...  102 us
    psum x1, waiting for transfers between devices, shards(): lax.psum((grad_conv_first, grad_conv_second, grad_conv_skip, grad_time_pr...  101 us
    dot_general x6, matrix products, project_back(): lax.dot_general(grads, matrix, (((grads.ndim - 1,), (1,)), ((), ())), pre...  47.4 us
    psum x1, blocking collectives, shards(): lax.psum((grad_conv_first, grad_conv_second, grad_conv_skip, grad_time_pr...  41.1 us
    dot_general x10, matrix products, project(): lax.dot_general(operand, matrix, (((operand.ndim - 1,), (0,)), ((), ())),...  28 us
    dot_general x1, matrix products, shards(): jnp.einsum('uqhd,ukhd->uhqk', grad_attended, values_all, preferred_elemen...  26.3 us
    dot_general x1, matrix products, attention_scores(): jnp.einsum('uqhd,ukhd->uhqk', queries, keys_all, preferred_element_type=j...  25.8 us
  transfers between devices with their start and end apart: 15, of which 5 were waited for; matrix products, arithmetic and copies ran while one was open for 46% of the time, Pallas kernels for 0%

commit v1 on v0

--- a/solution.py
+++ b/solution.py
@@ -1,7 +1,22 @@
+import functools
+import math
+
 import jax
 import jax.numpy as jnp
 from jax import lax
+from jax.experimental import pallas as pl
+from jax.experimental.pallas import tpu as pltpu
 from jax.sharding import PartitionSpec as P
+
+F32, BF = jnp.float32, jnp.bfloat16
+NT = (((1,), (1,)), ((), ()))
+NN = (((1,), (0,)), ((), ()))
+LOG2E = math.log2(math.e)
+
+
+def dot(a, b, dn=NN):
+    return lax.dot_general(a, b, dn, preferred_element_type=F32)
+
 
 HEADS = 2
 GROUPS = 8
@@ -123,6 +138,126 @@
     return values + jnp.square(jnp.sin(values * jnp.exp(snake_logs[0]))) / (
         jnp.exp(snake_logs[1]) + 1e-09
     )
+
+
+def fwd_kernel(QB, CK, len_ref, q_ref, k_ref, v_ref, o_ref, qa_ref, kb, vb):
+    u = pl.program_id(0)
+    W = k_ref.shape[1]; F = q_ref.shape[1]
+    L = len_ref[u]
+    lane = lax.broadcasted_iota(jnp.int32, (1, 128), 1)
+    first = lane < 64
+    c = 0.125 * LOG2E
+    nch = (L + CK - 1) // CK
+    one = jnp.ones((), BF)
+    for qi in range(F // QB):
+        q = q_ref[0, qi * QB:(qi + 1) * QB, :]
+        qh = [jnp.where(first, q, jnp.zeros_like(q)), jnp.where(first, jnp.zeros_like(q), q)]
+        def body(j, carry):
+            off = pl.multiple_of(j * CK, CK)
+            k = k_ref[0, pl.ds(off, CK), :]
+            v = v_ref[0, pl.ds(off, CK), :]
+            vh = [jnp.where(first, v, one), jnp.where(first, one, v)]
+            bias = jnp.where(off + lax.broadcasted_iota(jnp.int32, (1, CK), 1) < L, 0.0, -1e9)
+            out = []
+            for h in range(2):
+                m, acc = carry[h]
+                s = dot(qh[h], k, NT) + bias
+                mn = jnp.maximum(m, jnp.max(s, axis=1, keepdims=True))
+                p = jnp.exp2((s - mn) * c).astype(BF)
+                al = jnp.exp2((m - mn) * c)
+                acc = acc * al + dot(p, vh[h])
+                out.append((mn, acc))
+            return tuple(out)
+        init = tuple((jnp.full((QB, 1), -1e30, F32), jnp.zeros((QB, 128), F32)) for _ in range(2))
+        (m0, a0), (m1, a1) = lax.fori_loop(0, nch, body, init)
+        l0 = a0[:, 64:65]; l1 = a1[:, 0:1]
+        o_ref[0, qi * QB:(qi + 1) * QB, :] = jnp.where(first, a0 / l0, a1 / l1)
+        for h, (m, l) in enumerate(((m0, l0), (m1, l1))):
+            t = -(m + jnp.log2(l) / c)
+            t1 = t.astype(BF); r = t - t1.astype(F32); t2 = r.astype(BF); r = r - t2.astype(F32); t3 = r.astype(BF)
+            base = 64 * (1 - h)
+            qa = jnp.where(lane == base, t1, jnp.where(lane == base + 1, t2, jnp.where(lane == base + 2, t3,
+                 jnp.where(lane == base + 3, one, qh[h]))))
+            qa_ref[0, h, qi * QB:(qi + 1) * QB, :] = qa
+
+def attn_forward(lengths, q, k, v, QB=1024, CK=2048):
+    U, F, _ = q.shape; W = k.shape[1]
+    return pl.pallas_call(
+        functools.partial(fwd_kernel, QB, CK),
+        out_shape=(jax.ShapeDtypeStruct((U, F, 128), F32), jax.ShapeDtypeStruct((U, 2, F, 128), BF)),
+        grid_spec=pltpu.PrefetchScalarGridSpec(num_scalar_prefetch=1, grid=(U,),
+            in_specs=[pl.BlockSpec((1, F, 128), lambda u, _: (u, 0, 0)), pl.BlockSpec((1, W, 128), lambda u, _: (u, 0, 0)), pl.BlockSpec((1, W, 128), lambda u, _: (u, 0, 0))],
+            out_specs=[pl.BlockSpec((1, F, 128), lambda u, _: (u, 0, 0)), pl.BlockSpec((1, 2, F, 128), lambda u, _: (u, 0, 0, 0))],
+            scratch_shapes=[pltpu.VMEM((2, W, 128), BF), pltpu.VMEM((2, W, 128), BF)]),
+        compiler_params=pltpu.CompilerParams(vmem_limit_bytes=56 * 2**20), name="attn_fwd",
+    )(lengths, q, k, v)
+
+def bwd_kernel(KB, len_ref, qa_ref, da_ref, k_ref, v_ref, dq_ref, dk_ref, dv_ref, dqt):
+    u = pl.program_id(0)
+    W = k_ref.shape[1]; F = qa_ref.shape[2]
+    L = len_ref[u]
+    lane = lax.broadcasted_iota(jnp.int32, (1, 128), 1)
+    first = lane < 64
+    c = 0.125 * LOG2E
+    one = jnp.ones((), BF)
+    dqt[...] = jnp.zeros_like(dqt)
+    nkb = (L + KB - 1) // KB
+    def body(j, _):
+        off = pl.multiple_of(j * KB, KB)
+        k = k_ref[0, pl.ds(off, KB), :]
+        v = v_ref[0, pl.ds(off, KB), :]
+        kt = k.T
+        bias = jnp.where(off + lax.broadcasted_iota(jnp.int32, (KB, 1), 0) < L, 0.0, -1e9).astype(BF)
+        dvs, dks = [], []
+        for h in range(2):
+            base = 64 * (1 - h)
+            if h == 0:
+                ka = jnp.where(lane < 64, k, jnp.where(lane == base + 3, bias, jnp.where(lane < base + 3, one, 0 * one)))
+                va = jnp.where(lane < 64, v, jnp.where(lane < base + 3, -one, 0 * one))
+            else:
+                ka = jnp.where(lane >= 64, k, jnp.where(lane == base + 3, bias, jnp.where(lane < base + 3, one, 0 * one)))
+                va = jnp.where(lane >= 64, v, jnp.where(lane < base + 3, -one, 0 * one))
+            qa = qa_ref[0, h]
+            da = da_ref[0, h]
+            st = dot(ka, qa, NT)
+            p = jnp.exp2(st * c)
+            dp = dot(va, da, NT)
+            ds = (p * dp).astype(BF)
+            dvs.append(dot(p.astype(BF), da))
+            dks.append(dot(ds, qa))
+            dqt[h * 64:(h + 1) * 64, :] += dot(kt[h * 64:(h + 1) * 64, :], ds)
+        dk_ref[0, pl.ds(off, KB), :] = (jnp.where(first, dks[0], dks[1]) * 0.125).astype(BF)
+        dv_ref[0, pl.ds(off, KB), :] = jnp.where(first, dvs[0], dvs[1]).astype(BF)
+        return 0
+    lax.fori_loop(0, nkb, body, 0)
+    def zero(j, _):
+        off = pl.multiple_of(j * KB, KB)
+        dk_ref[0, pl.ds(off, KB), :] = jnp.zeros((KB, 128), BF)
+        dv_ref[0, pl.ds(off, KB), :] = jnp.zeros((KB, 128), BF)
+        return 0
+    lax.fori_loop(nkb, W // KB, zero, 0)
+    dq_ref[0] = (dqt[...] * 0.125).T.astype(BF)
+
+def attn_backward(lengths, qa, da, k, v, KB=512):
+    U, _, F, _ = qa.shape; W = k.shape[1]
+    return pl.pallas_call(
+        functools.partial(bwd_kernel, KB),
+        out_shape=(jax.ShapeDtypeStruct((U, F, 128), BF), jax.ShapeDtypeStruct((U, W, 128), BF), jax.ShapeDtypeStruct((U, W, 128), BF)),
+        grid_spec=pltpu.PrefetchScalarGridSpec(num_scalar_prefetch=1, grid=(U,),
+            in_specs=[pl.BlockSpec((1, 2, F, 128), lambda u, _: (u, 0, 0, 0)), pl.BlockSpec((1, 2, F, 128), lambda u, _: (u, 0, 0, 0)),
+                      pl.BlockSpec((1, W, 128), lambda u, _: (u, 0, 0)), pl.BlockSpec((1, W, 128), lambda u, _: (u, 0, 0))],
+            out_specs=[pl.BlockSpec((1, F, 128), lambda u, _: (u, 0, 0)), pl.BlockSpec((1, W, 128), lambda u, _: (u, 0, 0)), pl.BlockSpec((1, W, 128), lambda u, _: (u, 0, 0))],
+            scratch_shapes=[pltpu.VMEM((128, F), F32)]),
+        compiler_params=pltpu.CompilerParams(vmem_limit_bytes=56 * 2**20), name="attn_bwd",
+    )(lengths, qa, da, k, v)
+
+
+def split_bf16(t):
+    t1 = t.astype(BF)
+    r = t - t1.astype(F32)
+    t2 = r.astype(BF)
+    t3 = (r - t2.astype(F32)).astype(BF)
+    return jnp.stack([t1, t2, t3], axis=-1)
 
 
 def shards(
@@ -145,13 +280,10 @@
     snake_logs,
 ):
     utt_count, frame_count, channels = frames.shape
-    whole_len = frame_count * lax.axis_size("seq")
     inner_width = w_out.shape[0]
     head_dim = inner_width // HEADS
-    score_scale = head_dim ** (-0.5)
     positions = lax.axis_index("seq") * frame_count + jnp.arange(frame_count)
     frame_mask = (positions[None, :] < lengths[:, None]).astype(jnp.float32)
-    key_mask = jnp.arange(whole_len)[None, :] < lengths[:, None]
     counts = lengths.astype(jnp.float32) * (channels // GROUPS)
     column_mask = frame_mask[:, :, None]
     masked_in = frames * column_mask.astype(jnp.bfloat16)
@@ -174,23 +306,10 @@
         lax.all_gather(qkv_rows[:, :, inner_width : 2 * inner_width], "seq", axis=1, tiled=True),
         lax.all_gather(qkv_rows[:, :, 2 * inner_width :], "seq", axis=1, tiled=True),
     )
-    keys_all = keys_all.reshape(utt_count, whole_len, HEADS, head_dim)
-    values_all = values_all.reshape(utt_count, whole_len, HEADS, head_dim)
-
-    def attention_scores():
-        raw_scores = jnp.einsum(
-            "uqhd,ukhd->uhqk", queries, keys_all, preferred_element_type=jnp.float32
-        )
-        return jnp.where(key_mask[:, None, None, :], raw_scores * score_scale, -1000000000.0)
-
-    scores = attention_scores()
-    row_top = jnp.max(scores, axis=-1, keepdims=True)
-    log_total = row_top + jnp.log(jnp.sum(jnp.exp(scores - row_top), axis=-1, keepdims=True))
-    probs_low = jnp.exp(scores - log_total).astype(jnp.bfloat16)
-    attended = jnp.einsum(
-        "uhqk,ukhd->uqhd", probs_low, values_all, preferred_element_type=jnp.float32
-    )
-    attended = attended.astype(jnp.bfloat16).reshape(utt_count, frame_count, inner_width)
+    attended_full, queries_aug = attn_forward(
+        lengths, qkv_rows[:, :, :inner_width], keys_all, values_all
+    )
+    attended = attended_full.astype(BF)
     resid_two = resnet_out + project(attended, w_out) + shifts[7]
     normed_two = layer_norm(resid_two, gains[3], shifts[8]).astype(jnp.bfloat16)
     ff_hidden = project(normed_two, ff_in) + ff_bias
@@ -238,40 +357,29 @@
     grad_attn_low = grad_two.astype(jnp.bfloat16)
     grad_w_out = weight_grad(attended, grad_attn_low)
     grad_attended = project_back(grad_attn_low, w_out).astype(jnp.bfloat16)
-    grad_attended = grad_attended.reshape(utt_count, frame_count, HEADS, head_dim)
-    probs_full = jnp.exp(attention_scores() - log_total)
-    probs_again = probs_full.astype(jnp.bfloat16)
-    grad_probs = jnp.einsum(
-        "uqhd,ukhd->uhqk", grad_attended, values_all, preferred_element_type=jnp.float32
-    )
-    row_terms = jnp.sum(probs_full * grad_probs, axis=-1, keepdims=True)
-    grad_scores = (probs_full * (grad_probs - row_terms) * score_scale).astype(jnp.bfloat16)
-    grad_queries = jnp.einsum(
-        "uhqk,ukhd->uqhd", grad_scores, keys_all, preferred_element_type=jnp.float32
-    )
-    key_terms = jnp.einsum(
-        "uhqk,uqhd->ukhd", grad_scores, queries, preferred_element_type=jnp.float32
-    )
-    value_terms = jnp.einsum(
-        "uhqk,uqhd->ukhd", probs_again, grad_attended, preferred_element_type=jnp.float32
+    row_terms = jnp.sum(
+        (grad_attended.astype(F32) * attended_full).reshape(utt_count, frame_count, HEADS, head_dim),
+        axis=-1,
+    )
+    pieces = split_bf16(row_terms)
+    blank = jnp.zeros((utt_count, frame_count, head_dim - 3), BF)
+    grad_aug = jnp.stack(
+        [
+            jnp.concatenate([grad_attended[:, :, :head_dim], pieces[:, :, 0], blank], axis=-1),
+            jnp.concatenate([pieces[:, :, 1], blank, grad_attended[:, :, head_dim:]], axis=-1),
+        ],
+        axis=1,
+    )
+    grad_queries, key_terms, value_terms = attn_backward(
+        lengths, queries_aug, grad_aug, keys_all, values_all
     )
     grad_keys, grad_values = (
-        lax.psum_scatter(
-            key_terms.reshape(utt_count, whole_len, inner_width).astype(jnp.bfloat16),
-            "seq",
-            scatter_dimension=1,
-            tiled=True,
-        ).astype(jnp.float32),
-        lax.psum_scatter(
-            value_terms.reshape(utt_count, whole_len, inner_width).astype(jnp.bfloat16),
-            "seq",
-            scatter_dimension=1,
-            tiled=True,
-        ).astype(jnp.float32),
+        lax.psum_scatter(key_terms, "seq", scatter_dimension=1, tiled=True),
+        lax.psum_scatter(value_terms, "seq", scatter_dimension=1, tiled=True),
     )
     grad_qkv = jnp.concatenate(
-        [grad_queries.reshape(utt_count, frame_count, inner_width), grad_keys, grad_values], axis=2
-    ).astype(jnp.bfloat16)
+        [grad_queries, grad_keys, grad_values], axis=2
+    )
     grad_w_qkv = weight_grad(normed_one, grad_qkv)
     grad_normed_one = project_back(grad_qkv, w_qkv)
     outputs, norm_pull_one = jax.vjp(layer_norm, resnet_out, gains[2], shifts[6])

time: 766 us -> 561 us (0.73)
  matrix products: 403 us -> 94.4 us
  Pallas kernels: 0 us -> 73.9 us
  waiting for transfers between devices: 120 us -> 172 us
  other arithmetic: 56.2 us -> 34.9 us
    dot_general x6 -> x0, matrix products: 308 us -> none  [the longest x1 104 us: shards(): jnp.einsum('uhqk,uqhd->ukhd', grad_scores, queries, preferred_element_typ...]
    pallas_call x0 -> x2, Pallas kernels: none -> 73.9 us  [the longest x1 44.5 us: attn_backward(): pl.pallas_call(functools.partial(bwd_kernel, KB), out_shape=(jax.ShapeDty...]
    reduce_scatter x2, waiting for transfers between devices: 0.01 us -> 25.2 us  [the longest x1 25.2 us: shards(): lax.psum_scatter(value_terms, 'seq', scatter_dimension=1, tiled=True)]
    all_gather x1, waiting for transfers between devices: 0.02 us -> 24.8 us  [shards(): lax.all_gather(qkv_rows[:, :, 2 * inner_width:], 'seq', axis=1, tiled=True)]
    reduce_sum x1, other arithmetic: 21.4 us -> 1.31 us  [shards(): jnp.sum((grad_attended.astype(F32) * attended_full).reshape(utt_count, fr...]
    convert_element_type x3 -> x0, local copies, waits for them, and re-layouts: 8.7 us -> none  [the longest x1 4.08 us: shards(): value_terms.reshape(utt_count, whole_len, inner_width).astype(jnp.bfloat16)]
    unnamed x262 -> x237, local copies, waits for them, and re-layouts: 22.4 us -> 26.5 us
  transfers between devices with their start and end apart: 15 -> 15, of which waited for: 5 -> 7; matrix products, arithmetic and copies ran while one was open for 46% -> 11% of each run, Pallas kernels for 0% -> 0%
where the time goes in v1:
time: 561 us; the launch traced here: 551 us
  waiting for transfers between devices  172 us (31%)
  matrix products  94.4 us (17%)
  blocking collectives  74.1 us (13%)
  Pallas kernels  73.9 us (13%)
  local copies, waits for them, and re-layouts  56.8 us (10%)
  other arithmetic  34.9 us (6%)
  starting transfers between devices  29.5 us (5%)
  between operations  15.4 us (3%)
    psum x1, waiting for transfers between devices, shards(): lax.psum((grad_conv_first, grad_conv_second, grad_conv_skip, grad_time_pr...  102 us
    dot_general x6, matrix products, project_back(): lax.dot_general(grads, matrix, (((grads.ndim - 1,), (1,)), ((), ())), pre...  47.9 us
    pallas_call x1, Pallas kernels, attn_backward(): pl.pallas_call(functools.partial(bwd_kernel, KB), out_shape=(jax.ShapeDty...  44.5 us
    psum x1, blocking collectives, shards(): lax.psum((grad_conv_first, grad_conv_second, grad_conv_skip, grad_time_pr...  40.9 us
    pallas_call x1, Pallas kernels, attn_forward(): pl.pallas_call(functools.partial(fwd_kernel, QB, CK), out_shape=(jax.Shap...  29.4 us
    dot_general x10, matrix products, project(): lax.dot_general(operand, matrix, (((operand.ndim - 1,), (0,)), ((), ())),...  27.5 us
    unnamed x237, local copies, waits for them, and re-layouts  26.5 us
    reduce_scatter x1, waiting for transfers between devices, shards(): lax.psum_scatter(value_terms, 'seq', scatter_dimension=1, tiled=True)  25.2 us
  transfers between devices with their start and end apart: 15, of which 7 were waited for; matrix products, arithmetic and copies ran while one was open for 11% of the time, Pallas kernels for 0%

profile of v1, /device:TPU:1, one launch (start us, length us, event | category | flops | bytes accessed | tf_op | source)
XLA Modules:
  0.0 550.8 jit_solution(9481863764996350969)
XLA Ops:
  9.7 4.5 collective-permute-start
  22.0 5.1 psum.161
  27.9 6.0 %psum.162 = f32[2,8]{1,0:T(2,128)S(1)} all-reduce(f32[2,8]{1,0:T(2,128)S(1)} %reduce_sum.486), channel_id=1, replica_groups=mesh['dp'=8,'seq'=4] {'seq'}, use_global_device_ids=true, to_apply=%region_5.6 | all-reduce | flops 16 | bytes 128 | tf_op jit(solution)/shard_map/psum | solution.py:98
  36.5 3.9 collective-permute-start.2
  42.5 3.0 collective-permute-done.3
  48.2 5.2 psum.163
  54.2 6.0 %psum.164 = f32[2,8]{1,0:T(2,128)S(1)} all-reduce(f32[2,8]{1,0:T(2,128)S(1)} %reduce_sum.492), channel_id=1, replica_groups=mesh['dp'=8,'seq'=4] {'seq'}, use_global_device_ids=true, to_apply=%region_11.12 | all-reduce | flops 16 | bytes 128 | tf_op jit(solution)/shard_map/psum | solution.py:98
  61.0 3.4 fusion.127
  80.9 11.6 %all-gather.3.cloned.1.call-done.k_ref = bf16[2,4096,128]{2,1,0:T(8,128)(2,1)} async-done(((bf16[2,1024,128]{2,1,0:T(8,128)(2,1)}), bf16[2,4096,128]{2,1,0:T(8,128)(2,1)}) %all-gather.3.cloned.1.call-update) | async-done | bytes 2097168 | tf_op jit(solution)/shard_map/all_gather | solution.py:306
  92.5 24.8 %all-gather.5.cloned.1.call-done.v_ref = bf16[2,4096,128]{2,1,0:T(8,128)(2,1)} async-done(((bf16[2,1024,128]{2,1,0:T(8,128)(2,1)}), bf16[2,4096,128]{2,1,0:T(8,128)(2,1)}) %all-gather.5.cloned.1.call-update) | async-done | bytes 2097168 | tf_op jit(solution)/shard_map/all_gather | solution.py:307
  117.2 29.4 %attn_fwd.1 = (f32[2,1024,128]{2,1,0:T(8,128)}, bf16[2,2,1024,128]{3,2,1,0:T(8,128)(2,1)}) custom-call(s32[2]{0:T(128)} %len_ref.3, bf16[2,1024,128]{2,1,0:T(8,128)(2,1)} %get-tuple-element.92.q_ref, bf16[2,4096,128]{2,1,0:T(8,128)(2,1)} %all-gather.3.cloned.1.call-done.k_ref, bf16[2,4096,128]{2,1,0:T(8,128)(2,1)} %all-gather.5.cloned.1.call-done.v_ref), custom_call_target="tpu_custom_call" | custom-call | tf_op jit(solution)/shard_map/attn_fwd/pallas_call | solution.py:185
  151.1 38.7 %multiply_reduce_fusion.1 = (f32[1024]{0:T(1024)}, f32[1024]{0:T(1024)}, f32[1024]{0:T(1024)}, bf16[2,1024,1024]{2,1,0:T(8,128)(2,1)S(1)}, bf16[2,1024,1024]{2,1,0:T(8,128)(2,1)}) fusion(f32[2,1024,1024]{2,1,0:T(8,128)S(1)} %fusion.71, f32[1024]{0:T(1024)S(1)} %multiply_divide_fusion, f32[1024]{0:T(1024)S(1)} %bitcast.250, f32[1024]{0:T(1024)S(1)} %copy-done.107, ...), kind=kOutput, calls=%fused_computation.2 | convolution fusion | flops 1114633216 | bytes 19435520 | tf_op jit(solution)/shard_map/dot_general | solution.py:58
  208.5 44.5 %attn_bwd.1 = (bf16[2,1024,128]{2,1,0:T(8,128)(2,1)}, bf16[2,4096,128]{2,1,0:T(8,128)(2,1)}, bf16[2,4096,128]{2,1,0:T(8,128)(2,1)}) custom-call(s32[2]{0:T(128)} %len_ref.3, bf16[2,2,1024,128]{3,2,1,0:T(8,128)(2,1)} %get-tuple-element.25.qa_ref, bf16[2,2,1024,128]{3,2,1,0:T(8,128)(2,1)} %pad_maximum_fusion.9.da_ref, ...), custom_call_target="tpu_custom_call" | custom-call | tf_op jit(solution)/shard_map/attn_bwd/pallas_call | solution.py:243
  255.0 4.7 copy.91
  259.7 4.8 copy.92
  264.6 4.4 multiply_convert_fusion
  274.1 3.1 convolution_bitcast_fusion.3
  281.6 2.8 fusion.51
  288.0 3.0 fusion.132
  292.9 25.2 %reduce-scatter.5.cloned.1.call-done = bf16[2,1024,128]{2,1,0:T(8,128)(2,1)} async-done(((bf16[2,4096,128]{2,1,0:T(8,128)(2,1)}), bf16[2,1024,128]{2,1,0:T(8,128)(2,1)}) %reduce-scatter.5.cloned.1.call-update) | async-done | bytes 524304 | tf_op jit(solution)/shard_map/reduce_scatter | solution.py:378
  320.2 2.9 fusion.109
  328.7 4.2 multiply_reduce_fusion.5
  333.2 5.7 %all-reduce.5 = (f32[2,8]{1,0:T(2,128)S(1)}, f32[2,8]{1,0:T(2,128)S(1)}) all-reduce(f32[2,8]{1,0:T(2,128)S(1)} %reduce_sum.508, f32[2,8]{1,0:T(2,128)S(1)} %neg.47), channel_id=1, replica_groups=mesh['dp'=8,'seq'=4] {'seq'}, use_global_device_ids=true, to_apply=%region_28.30 | all-reduce | flops 32 | bytes 256 | tf_op jit(solution)/shard_map/psum | solution.py:119
  344.4 3.4 collective-permute-start.7
  351.5 5.9 %multiply_reduce_fusion.6 = (f32[256]{0:T(256)S(1)}, f32[2,256]{1,0:T(2,128)S(1)}, f32[2,256]{1,0:T(2,128)S(1)}, f32[256]{0:T(256)S(1)}, f32[2,1024,256]{2,1,0:T...) fusion(f32[2,256]{1,0:T(2,128)S(1)} %copy-done.68, f32[2,256]{1,0:T(2,128)S(1)} %copy-done.60, ...), kind=kOutput, calls=%fused_computation.52 | convolution fusion | flops 839383296 | bytes 7757824 | tf_op jit(solution)/shard_map/dot_general | solution.py:52
  357.8 5.1 all-reduce.4
  363.3 3.1 fusion.113
  378.7 3.0 collective-permute-start.8
  381.8 3.1 collective-permute-start.9
  384.9 40.9 %all-reduce.2 = (f32[2,256]{1,0:T(2,128)S(1)}, f32[2,256]{1,0:T(2,128)S(1)}, f32[5,256]{1,0:T(8,128)S(1)}, f32[6,256]{1,0:T(8,128)S(1)}, f32[1024]{0:T(1024)}, /*index=5*/f32[2,1024]{1,0:T(2,128)}) all-reduce(f32[2,256]{1,0:T(2,128)S(1)} %get-tuple-element.148, ...), channel_id=1, replica_groups=mesh['dp'=8,'seq'=4] {'dp','seq'}, use_global_device_ids=true, to_apply=%region_51.53 | all-reduce | flops 6912 | bytes 55296 | tf_op jit(solution)/shard_map/psum | solution.py:438
  427.0 5.2 add_multiply_fusion
  432.2 101.6 %all-reduce.8.cloned.1.call-done = (f32[3,256,256]{2,1,0:T(8,128)}, f32[3,256,256]{2,1,0:T(8,128)}, f32[256,256]{1,0:T(8,128)}, f32[1024,256]{1,0:T(8,128)}, f32...) async-done(((f32[3,256,256]{2,1,0:T(8,128)}, f32[3,256,256]{2,1,0:T(8,128)}, ...) | async-done | bytes 6291472 | tf_op jit(solution)/shard_map/psum | solution.py:438
  (388 shorter events, 116.9 us)
Async XLA Ops:
  7.2 143.6 %copy-start = (bf16[1024,256]{1,0:T(8,128)(2,1)S(1)}, bf16[1024,256]{1,0:T(8,128)(2,1)}, u32[]{:S(2)}) copy-start(bf16[1024,256]{1,0:T(8,128)(2,1)} %param.29) | copy-start | bytes 1572868
  7.2 85.2 %all-gather.3.cloned.1.call-start = ((), (), s32[]{:S(2)}) async-start(), calls=%async_computation.2 | async-start | bytes 2621440 | tf_op jit(solution)/shard_map/all_gather | solution.py:306
  9.7 7.4 %collective-permute-start = (bf16[2,1,256]{2,1,0:T(2,128)(2,1)S(1)}, bf16[2,1,256]{2,1,0:T(2,128)(2,1)S(1)}, u32[]{:S(2)}, u32[]{:S(2)}) collective-permute-start(bf16[2,1,256]{2,1,0:T(2,128)(2,1)S(1)} %get-tuple-element.101), channel_id=1, source_target_pairs={{0,1},{1,2},{2,3},{4,5},{5,6},{6,7},{8,9},{9,10},{10,11},{12,13},{... | collective-permute-start | bytes 3080 | tf_op jit(solution)/shard_map/ppermute | solution.py:35
  14.3 4.9 collective-permute-start.1
  16.8 17.8 %copy-start.73 = (f32[1,256]{1,0:T(1,128)}, f32[1,256]{1,0:T(1,128)S(1)}, u32[]{:S(2)}) copy-start(f32[1,256]{1,0:T(1,128)S(1)} %get-tuple-element.122) | copy-start | bytes 3076
  16.8 17.8 %copy-start.87 = (f32[1,256]{1,0:T(1,128)}, f32[1,256]{1,0:T(1,128)S(1)}, u32[]{:S(2)}) copy-start(f32[1,256]{1,0:T(1,128)S(1)} %get-tuple-element.121) | copy-start | bytes 3076
  16.8 44.2 %copy-start.75 = (f32[1,256]{1,0:T(1,128)}, f32[1,256]{1,0:T(1,128)S(1)}, u32[]{:S(2)}) copy-start(f32[1,256]{1,0:T(1,128)S(1)} %get-tuple-element.119) | copy-start | bytes 3076
  16.8 44.2 %copy-start.89 = (f32[1,256]{1,0:T(1,128)}, f32[1,256]{1,0:T(1,128)S(1)}, u32[]{:S(2)}) copy-start(f32[1,256]{1,0:T(1,128)S(1)} %get-tuple-element.118) | copy-start | bytes 3076
  16.8 48.3 %copy-start.91 = (f32[1,256]{1,0:T(1,128)}, f32[1,256]{1,0:T(1,128)S(1)}, u32[]{:S(2)}) copy-start(f32[1,256]{1,0:T(1,128)S(1)} %get-tuple-element.116) | copy-start | bytes 3076
  16.8 132.3 %copy-start.61 = (f32[1,256]{1,0:T(1,128)}, f32[1,256]{1,0:T(1,128)S(1)}, u32[]{:S(2)}) copy-start(f32[1,256]{1,0:T(1,128)S(1)} %get-tuple-element.114) | copy-start | bytes 3076
  16.8 17.8 %copy-start.81 = (f32[1,256]{1,0:T(1,128)}, f32[1,256]{1,0:T(1,128)S(1)}, u32[]{:S(2)}) copy-start(f32[1,256]{1,0:T(1,128)S(1)} %get-tuple-element.132) | copy-start | bytes 3076
  16.8 44.1 %copy-start.83 = (f32[1,256]{1,0:T(1,128)}, f32[1,256]{1,0:T(1,128)S(1)}, u32[]{:S(2)}) copy-start(f32[1,256]{1,0:T(1,128)S(1)} %get-tuple-element.131) | copy-start | bytes 3076
  16.9 48.3 %copy-start.63 = (f32[1,256]{1,0:T(1,128)}, f32[1,256]{1,0:T(1,128)S(1)}, u32[]{:S(2)}) copy-start(f32[1,256]{1,0:T(1,128)S(1)} %get-tuple-element.133) | copy-start | bytes 3076
  21.8 14.6 %copy-start.11 = (f32[2,1024,256]{2,1,0:T(8,128)}, f32[2,1024,256]{2,1,0:T(8,128)S(1)}, u32[]{:S(2)}) copy-start(f32[2,1024,256]{2,1,0:T(8,128)S(1)} %get-tuple-element.135) | copy-start | bytes 6291460
  36.5 6.0 %collective-permute-start.2 = (bf16[2,1,256]{2,1,0:T(2,128)(2,1)S(1)}, bf16[2,1,256]{2,1,0:T(2,128)(2,1)S(1)}, u32[]{:S(2)}, u32[]{:S(2)}) collective-permute-start(bf16[2,1,256]{2,1,0:T(2,128)(2,1)S(1)} %get-tuple-element.99), channel_id=1, source_target_pairs={{0,1},{1,2},{2,3},{4,5},{5,6},{6,7},{8,9},{9,10},{10,11},{12,13},{... | collective-permute-start | bytes 3080 | tf_op jit(solution)/shard_map/ppermute | solution.py:35
  40.4 5.0 collective-permute-start.3
  48.0 16.4 %copy-start.8 = (f32[2,1024,256]{2,1,0:T(8,128)}, f32[2,1024,256]{2,1,0:T(8,128)S(1)}, u32[]{:S(2)}) copy-start(f32[2,1024,256]{2,1,0:T(8,128)S(1)} %get-tuple-element.137) | copy-start | bytes 6291460
  67.9 49.3 %all-gather.5.cloned.1.call-start = ((), (), s32[]{:S(2)}) async-start(), calls=%async_computation.3 | async-start | bytes 2621440 | tf_op jit(solution)/shard_map/all_gather | solution.py:307
  68.6 222.4 %reduce-scatter.3.cloned.1.call-start = ((), (), s32[]{:S(2)}) async-start(), calls=%async_computation.4 | async-start | bytes 2621440 | tf_op jit(solution)/shard_map/reduce_scatter | solution.py:377
  70.4 5.2 collective-permute-start.5
  117.2 29.4 %copy-start.2 = (f32[2,1024,256]{2,1,0:T(8,128)S(1)}, f32[2,1024,256]{2,1,0:T(8,128)}, u32[]{:S(2)}) copy-start(f32[2,1024,256]{2,1,0:T(8,128)} %copy-done.1) | copy-start | bytes 6291460
  117.2 29.4 %copy-start.51 = (bf16[128,256]{1,0:T(8,128)(2,1)S(1)}, bf16[128,256]{1,0:T(8,128)(2,1)}, u32[]{:S(2)}) copy-start(bf16[128,256]{1,0:T(8,128)(2,1)} %param.27) | copy-start | bytes 196612
  253.1 65.1 %reduce-scatter.5.cloned.1.call-start = ((), (), s32[]{:S(2)}) async-start(), calls=%async_computation.5 | async-start | bytes 2621440 | tf_op jit(solution)/shard_map/reduce_scatter | solution.py:378
  253.6 280.2 %all-reduce.8.cloned.1.call-start = ((), (), s32[]{:S(2)}) async-start(), calls=%async_computation.6 | async-start | bytes 12582912 | tf_op jit(solution)/shard_map/psum | solution.py:438
  272.0 13.6 %collective-permute-start.4 = (bf16[2,1,256]{2,1,0:T(2,128)(2,1)S(1)}, bf16[2,1,256]{2,1,0:T(2,128)(2,1)S(1)}, u32[]{:S(2)}, u32[]{:S(2)}) collective-permute-start(bf16[2,1,256]{2,1,0:T(2,128)(2,1)S(1)} %slice.222), channel_id=1, source_target_pairs={{0,1},{1,2},{2,3},{4,5},{5,6},{6,7},{8,9},{9,10},{10,11},{12,13},{... | collective-permute-start | bytes 3080 | tf_op jit(solution)/shard_map/ppermute | solution.py:44
  288.0 32.2 %copy-start.3 = (f32[2,1024,256]{2,1,0:T(8,128)S(1)}, f32[2,1024,256]{2,1,0:T(8,128)}, u32[]{:S(2)}) copy-start(f32[2,1024,256]{2,1,0:T(8,128)} %copy-done.1) | copy-start | bytes 6291460
  288.0 32.2 %copy-start.64 = (f32[1,256]{1,0:T(1,128)S(1)}, f32[1,256]{1,0:T(1,128)}, u32[]{:S(2)}) copy-start(f32[1,256]{1,0:T(1,128)} %copy-done.63) | copy-start | bytes 3076
  341.8 9.2 %collective-permute-start.6 = (bf16[2,1,256]{2,1,0:T(2,128)(2,1)S(1)}, bf16[2,1,256]{2,1,0:T(2,128)(2,1)S(1)}, u32[]{:S(2)}, u32[]{:S(2)}) collective-permute-start(bf16[2,1,256]{2,1,0:T(2,128)(2,1)S(1)} %get-tuple-element.95), channel_id=1, source_target_pairs={{1,0},{2,1},{3,2},{5,4},{6,5},{7,6},{9,8},{10,9},{11,10},{13,12},{... | collective-permute-start | bytes 3080 | tf_op jit(solution)/shard_map/ppermute | solution.py:36
  344.4 6.6 %collective-permute-start.7 = (bf16[2,1,256]{2,1,0:T(2,128)(2,1)S(1)}, bf16[2,1,256]{2,1,0:T(2,128)(2,1)S(1)}, u32[]{:S(2)}, u32[]{:S(2)}) collective-permute-start(bf16[2,1,256]{2,1,0:T(2,128)(2,1)S(1)} %get-tuple-element.96), channel_id=1, source_target_pairs={{0,1},{1,2},{2,3},{4,5},{5,6},{6,7},{8,9},{9,10},{10,11},{12,13},{... | collective-permute-start | bytes 3080 | tf_op jit(solution)/shard_map/ppermute | solution.py:35
  376.2 50.9 %copy-start.49 = (bf16[3,256,256]{1,2,0:T(8,128)(2,1)S(1)}, bf16[3,256,256]{1,2,0:T(8,128)(2,1)}, u32[]{:S(2)}) copy-start(bf16[3,256,256]{1,2,0:T(8,128)(2,1)} %copy.90) | copy-start | bytes 1179652
  378.7 48.3 %collective-permute-start.8 = (bf16[2,1,256]{2,1,0:T(2,128)(2,1)S(1)}, bf16[2,1,256]{2,1,0:T(2,128)(2,1)S(1)}, u32[]{:S(2)}, u32[]{:S(2)}) collective-permute-start(bf16[2,1,256]{2,1,0:T(2,128)(2,1)S(1)} %get-tuple-element.93), channel_id=1, source_target_pairs={{1,0},{2,1},{3,2},{5,4},{6,5},{7,6},{9,8},{10,9},{11,10},{13,12},{... | collective-permute-start | bytes 3080 | tf_op jit(solution)/shard_map/ppermute | solution.py:36
  381.8 45.3 %collective-permute-start.9 = (bf16[2,1,256]{2,1,0:T(2,128)(2,1)S(1)}, bf16[2,1,256]{2,1,0:T(2,128)(2,1)S(1)}, u32[]{:S(2)}, u32[]{:S(2)}) collective-permute-start(bf16[2,1,256]{2,1,0:T(2,128)(2,1)S(1)} %get-tuple-element.94), channel_id=1, source_target_pairs={{0,1},{1,2},{2,3},{4,5},{5,6},{6,7},{8,9},{9,10},{10,11},{12,13},{... | collective-permute-start | bytes 3080 | tf_op jit(solution)/shard_map/ppermute | solution.py:35
  (92 other events, 351.0 us)
Sparse Core Ops, SparseCore 0:
  68.0 24.4 all-gather.2
  94.6 22.5 all-gather.4
  253.2 30.9 reduce-scatter.2
  286.7 31.3 reduce-scatter.4
  370.3 163.4 all-reduce.7

commit v2 on v1

--- a/solution.py
+++ b/solution.py
@@ -12,6 +12,7 @@
 NT = (((1,), (1,)), ((), ()))
 NN = (((1,), (0,)), ((), ()))
 LOG2E = math.log2(math.e)
+MESH = pl.DeviceIdType.MESH
 
 
 def dot(a, b, dn=NN):
@@ -260,6 +261,136 @@
     return jnp.stack([t1, t2, t3], axis=-1)
 
 
+def butterfly(axes):
+    hops = []
+    for axis, size in axes:
+        place = lax.axis_index(axis)
+        bit = 1
+        while bit < size:
+            up = (place // bit) % 2
+            hops.append((axis, place + bit - 2 * bit * up, up))
+            bit *= 2
+    return hops
+
+
+def orders(count):
+    plain = list(range(count))
+    if count < 5:
+        return [plain] * 3
+    tail = plain[4:]
+    return [plain, [0, 2, 3, 1] + tail, [0, 3, 1, 2] + tail]
+
+
+def greet(hops):
+    barrier = pltpu.get_barrier_semaphore()
+    for axis, partner, _ in hops:
+        pl.semaphore_signal(barrier, inc=1, device_id={axis: partner}, device_id_type=MESH)
+    pl.semaphore_wait(barrier, len(hops))
+
+
+def reduce_kernel(axes, count, refs_n, *refs):
+    ins, small_in = refs[:refs_n], refs[refs_n]
+    outs, small_out = refs[refs_n + 1 : 2 * refs_n + 1], refs[2 * refs_n + 1]
+    total, sent, got, whole, small_got, sems, small_sems = refs[2 * refs_n + 2 :]
+    hops = butterfly(axes)
+    greet(hops)
+    rows_all = total.shape[0]
+    part = rows_all // 3
+    plans = orders(count)
+
+    def copy(src, dst, hop, send, recv):
+        axis, partner, _ = hops[hop]
+        return pltpu.make_async_remote_copy(
+            src, dst, send, recv, device_id={axis: partner}, device_id_type=MESH
+        )
+
+    row = 0
+    for ref in ins:
+        rows, columns = ref.shape
+        for column in range(0, columns, 128):
+            total[pl.ds(row, rows), :] = ref[:, column : column + 128]
+            row += rows
+    lows = [None] * 3
+    small_out[...] = small_in[...]
+    for phase in range(count):
+        length = part >> (phase + 1)
+        copies = []
+        for p in range(3):
+            hop = plans[p][phase]
+            up = hops[hop][2]
+            start = p * part if phase == 0 else lows[p]
+            keep = pl.multiple_of(start + up * length, 16)
+            give = pl.multiple_of(start + (1 - up) * length, 16)
+            lows[p] = keep
+            at = p * part + part - (part >> phase)
+            slot = pl.ds(at, length)
+            sent[slot, :] = total[pl.ds(give, length), :].astype(BF)
+            sem = p * count + phase
+            go = copy(sent.at[slot], got.at[slot], hop, sems.at[0, sem], sems.at[1, sem])
+            go.start()
+            copies.append((go, slot, keep))
+        small = copy(
+            small_out, small_got.at[phase], phase, small_sems.at[0, phase], small_sems.at[1, phase]
+        )
+        small.start()
+        for go, slot, keep in copies:
+            go.wait()
+            total[pl.ds(keep, length), :] += got[slot, :].astype(F32)
+        small.wait()
+        small_out[...] += small_got[phase]
+    length = part >> count
+    for p in range(3):
+        whole[pl.ds(lows[p], length), :] = total[pl.ds(lows[p], length), :].astype(BF)
+    for phase in range(count - 1, -1, -1):
+        length = part >> (phase + 1)
+        copies = []
+        for p in range(3):
+            hop = plans[p][phase]
+            up = hops[hop][2]
+            here = pl.ds(lows[p], length)
+            sem = (3 + p) * count + phase
+            go = copy(whole.at[here], whole.at[here], hop, sems.at[0, sem], sems.at[1, sem])
+            go.start()
+            copies.append(go)
+            lows[p] = pl.multiple_of(lows[p] - up * length, 16)
+        for go in copies:
+            go.wait()
+    row = 0
+    for ref in outs:
+        rows, columns = ref.shape
+        for column in range(0, columns, 128):
+            ref[:, column : column + 128] = whole[pl.ds(row, rows), :].astype(F32)
+            row += rows
+
+
+def reduce_all(mats, small, axes):
+    count = sum(size.bit_length() - 1 for _, size in axes)
+    rows = sum(m.shape[0] * m.shape[1] // 128 for m in mats)
+    unit = 3 * 16 << count
+    padded = -(-rows // unit) * unit
+    vmem = pl.BlockSpec(memory_space=pltpu.VMEM)
+    out = pl.pallas_call(
+        functools.partial(reduce_kernel, axes, count, len(mats)),
+        out_shape=tuple(jax.ShapeDtypeStruct(m.shape, F32) for m in [*mats, small]),
+        in_specs=[vmem] * (len(mats) + 1),
+        out_specs=[vmem] * (len(mats) + 1),
+        scratch_shapes=[
+            pltpu.VMEM((padded, 128), F32),
+            pltpu.VMEM((padded, 128), BF),
+            pltpu.VMEM((padded, 128), BF),
+            pltpu.VMEM((padded, 128), BF),
+            pltpu.VMEM((count, *small.shape), F32),
+            pltpu.SemaphoreType.DMA((2, 6 * count)),
+            pltpu.SemaphoreType.DMA((2, count)),
+        ],
+        compiler_params=pltpu.CompilerParams(
+            collective_id=0, has_side_effects=True, vmem_limit_bytes=58 * 2**20
+        ),
+        name="reduce_weights",
+    )(*mats, small)
+    return out[:-1], out[-1]
+
+
 def shards(
     frames,
     time_embed,
@@ -435,30 +566,48 @@
             grad_shift_skip,
         ]
     )
-    summed = lax.psum(
-        (
-            grad_conv_first,
-            grad_conv_second,
-            grad_conv_skip,
-            grad_time_proj,
-            lower_gains,
-            lower_shifts,
-            upper_sums[0],
-            upper_sums[1],
-            upper_sums[2],
-            upper_sums[3],
-            upper_sums[4],
+    axes = (("seq", lax.axis_size("seq")), ("dp", lax.axis_size("dp")))
+    small = jnp.concatenate(
+        [
+            *lower_gains,
+            *upper_sums[7],
+            *lower_shifts,
+            *upper_sums[8],
             upper_sums[5],
-            upper_sums[6],
-            upper_sums[7],
-            upper_sums[8],
-        ),
-        ("dp", "seq"),
-    )
-    lower_sums = summed[:6]
-    upper_sums = summed[6:]
-    grad_gains = jnp.concatenate([lower_sums[4], upper_sums[7]], axis=0)
-    grad_shifts = jnp.concatenate([lower_sums[5], upper_sums[8]], axis=0)
+            *upper_sums[6],
+            jnp.zeros((5 * channels,), F32),
+        ]
+    ).reshape(-1, channels)
+    mats = [
+        grad_conv_first.reshape(-1, channels),
+        grad_conv_second.reshape(-1, channels),
+        grad_conv_skip,
+        grad_time_proj,
+        grad_w_qkv,
+        grad_w_out,
+        grad_ff_in,
+        grad_ff_out,
+        grad_conv_down.reshape(-1, channels),
+    ]
+    summed, small = reduce_all(mats, small, axes)
+    hidden = grad_ff_bias.shape[0]
+    grad_gains, grad_shifts = small[:4], small[4:15]
+    flat = small[15:].reshape(-1)
+    lower_sums = (
+        summed[0].reshape(conv_first.shape),
+        summed[1].reshape(conv_second.shape),
+        summed[2],
+        summed[3],
+    )
+    upper_sums = (
+        summed[8].reshape(conv_down.shape),
+        summed[4],
+        summed[5],
+        summed[6],
+        summed[7],
+        flat[:hidden],
+        flat[hidden : 3 * hidden].reshape(2, hidden),
+    )
     return (
         layer_out,
         grad_frames,

time: 561 us -> 474 us (0.84)
  waiting for transfers between devices: 172 us -> 65.7 us
  Pallas kernels: 73.9 us -> 135 us
  blocking collectives: 74.1 us -> 33.1 us
  matrix products: 94.4 us -> 102 us
  local copies, waits for them, and re-layouts: 56.8 us -> 49.5 us
    psum x1 -> x0, waiting for transfers between devices: 102 us -> none  [shards(): lax.psum((grad_conv_first, grad_conv_second, grad_conv_skip, grad_time_pr...]
    pallas_call x0 -> x1, Pallas kernels: none -> 61 us  [reduce_all(): pl.pallas_call(functools.partial(reduce_kernel, axes, count, len(mats)),...]
    psum x1 -> x0, blocking collectives: 40.9 us -> none  [shards(): lax.psum((grad_conv_first, grad_conv_second, grad_conv_skip, grad_time_pr...]
    dot_general x10, matrix products: 27.5 us -> 67.9 us  [project(): lax.dot_general(operand, matrix, (((operand.ndim - 1,), (0,)), ((), ())),...]
    dot_general x6, matrix products: 47.9 us -> 15.8 us  [project_back(): lax.dot_general(grads, matrix, (((grads.ndim - 1,), (1,)), ((), ())), pre...]
    dot_general x3 -> x0, local copies, waits for them, and re-layouts: 11.2 us -> none  [weight_grad(): lax.dot_general(flat_operand, flat_grads, (((0,), (0,)), ((), ())), prefe...]
    all_gather x1, waiting for transfers between devices: 11.6 us -> 2.34 us  [shards(): lax.all_gather(qkv_rows[:, :, inner_width:2 * inner_width], 'seq', axis=1...]
    unnamed x237 -> x263, local copies, waits for them, and re-layouts: 26.5 us -> 24.3 us
  transfers between devices with their start and end apart: 15 -> 14, of which waited for: 7 -> 6; matrix products, arithmetic and copies ran while one was open for 11% -> 11% of each run, Pallas kernels for 0% -> 0%
where the time goes in v2:
time: 474 us; the launch traced here: 465 us
  Pallas kernels  135 us (28%)
  matrix products  102 us (22%)
  waiting for transfers between devices  65.7 us (14%)
  local copies, waits for them, and re-layouts  49.5 us (10%)
  other arithmetic  35.8 us (8%)
  blocking collectives  33.1 us (7%)
  starting transfers between devices  28.9 us (6%)
  between operations  15.7 us (3%)
    dot_general x10, matrix products, project(): lax.dot_general(operand, matrix, (((operand.ndim - 1,), (0,)), ((), ())),...  67.9 us
    pallas_call x1, Pallas kernels, reduce_all(): pl.pallas_call(functools.partial(reduce_kernel, axes, count, len(mats)),...  61 us
    pallas_call x1, Pallas kernels, attn_backward(): pl.pallas_call(functools.partial(bwd_kernel, KB), out_shape=(jax.ShapeDty...  44.6 us
    reduce_scatter x1, waiting for transfers between devices, shards(): lax.psum_scatter(value_terms, 'seq', scatter_dimension=1, tiled=True)  30.6 us
    pallas_call x1, Pallas kernels, attn_forward(): pl.pallas_call(functools.partial(fwd_kernel, QB, CK), out_shape=(jax.Shap...  29.4 us
    all_gather x1, waiting for transfers between devices, shards(): lax.all_gather(qkv_rows[:, :, 2 * inner_width:], 'seq', axis=1, tiled=True)  24.8 us
    unnamed x263, local copies, waits for them, and re-layouts  24.3 us
    dot_general x8, matrix products, weight_grad(): lax.dot_general(flat_operand, flat_grads, (((0,), (0,)), ((), ())), prefe...  17.8 us
  transfers between devices with their start and end apart: 14, of which 6 were waited for; matrix products, arithmetic and copies ran while one was open for 11% of the time, Pallas kernels for 0%

profile of v2, /device:TPU:1, one launch (start us, length us, event | category | flops | bytes accessed | tf_op | source)
XLA Modules:
  0.0 465.4 jit_solution(18589802337229506)
XLA Ops:
  9.8 4.5 collective-permute-start
  20.8 5.1 %psum.56 = f32[2,8]{1,0:T(2,128)S(1)} all-reduce(f32[2,8]{1,0:T(2,128)S(1)} %reduce_sum.483), channel_id=1, replica_groups=mesh['dp'=8,'seq'=4] {'seq'}, use_global_device_ids=true, to_apply=%region_2.0 | all-reduce | flops 16 | bytes 128 | tf_op jit(solution)/shard_map/psum | solution.py:96
  26.7 6.0 %psum.57 = f32[2,8]{1,0:T(2,128)S(1)} all-reduce(f32[2,8]{1,0:T(2,128)S(1)} %reduce_sum.486), channel_id=1, replica_groups=mesh['dp'=8,'seq'=4] {'seq'}, use_global_device_ids=true, to_apply=%region_5.6 | all-reduce | flops 16 | bytes 128 | tf_op jit(solution)/shard_map/psum | solution.py:99
  35.3 3.9 collective-permute-start.2
  41.2 3.0 collective-permute-done.3
  45.7 5.2 %psum.58 = f32[2,8]{1,0:T(2,128)S(1)} all-reduce(f32[2,8]{1,0:T(2,128)S(1)} %reduce_sum.489), channel_id=1, replica_groups=mesh['dp'=8,'seq'=4] {'seq'}, use_global_device_ids=true, to_apply=%region_8.9 | all-reduce | flops 16 | bytes 128 | tf_op jit(solution)/shard_map/psum | solution.py:96
  51.7 6.0 %psum.59 = f32[2,8]{1,0:T(2,128)S(1)} all-reduce(f32[2,8]{1,0:T(2,128)S(1)} %reduce_sum.492), channel_id=1, replica_groups=mesh['dp'=8,'seq'=4] {'seq'}, use_global_device_ids=true, to_apply=%region_11.12 | all-reduce | flops 16 | bytes 128 | tf_op jit(solution)/shard_map/psum | solution.py:99
  58.5 4.1 fusion.127
  74.8 3.0 copy.83
  77.7 4.1 reshape.420
  81.8 6.2 %fusion.58 = f32[2,1024,1024]{2,1,0:T(8,128)} fusion(bf16[1024,256]{1,0:T(8,128)(2,1)} %param.29, f32[2,1024,256]{2,1,0:T(8,128)} %reshape.420, f32[2,1024]{1,0:T(2,128)S(1)} %get-tuple-element.136), kind=kOutput, calls=%fused_computation.131 | convolution fusion | flops 1074790400 | bytes 11018240 | tf_op jit(solution)/shard_map/dot_general | solution.py:59
  90.4 24.8 %all-gather.5.cloned.1.call-done.v_ref = bf16[2,4096,128]{2,1,0:T(8,128)(2,1)} async-done(((bf16[2,1024,128]{2,1,0:T(8,128)(2,1)}), bf16[2,4096,128]{2,1,0:T(8,128)(2,1)}) %all-gather.5.cloned.1.call-update) | async-done | bytes 2097168 | tf_op jit(solution)/shard_map/all_gather | solution.py:438
  115.2 29.4 %attn_fwd.1 = (f32[2,1024,128]{2,1,0:T(8,128)}, bf16[2,2,1024,128]{3,2,1,0:T(8,128)(2,1)}) custom-call(s32[2]{0:T(128)} %len_ref.3, bf16[2,1024,128]{2,1,0:T(8,128)(2,1)} %get-tuple-element.97.q_ref, bf16[2,4096,128]{2,1,0:T(8,128)(2,1)} %all-gather.3.cloned.1.call-done.k_ref, bf16[2,4096,128]{2,1,0:T(8,128)(2,1)} %all-gather.5.cloned.1.call-done.v_ref), custom_call_target="tpu_custom_call" | custom-call | tf_op jit(solution)/shard_map/attn_fwd/pallas_call | solution.py:186
  147.2 40.9 %multiply_reduce_fusion = (f32[1024]{0:T(1024)}, f32[1024]{0:T(1024)}, f32[1024]{0:T(1024)}, bf16[2,1024,1024]{2,1,0:T(8,128)(2,1)S(1)}, bf16[2,1024,1024]{2,1,0:T(8,128)(2,1)}) fusion(f32[1024]{0:T(1024)S(1)} %copy-done.104, f32[1024]{0:T(1024)S(1)} %bitcast.205, f32[2,1024,1024]{2,1,0:T(8,128)} %fusion.58, f32[1024]{0:T(1024)S(1)} %bitcast.175, ...), kind=kOutput, calls=%fused_computation.1 | convolution fusion | flops 1116206080 | bytes 19445760 | tf_op jit(solution)/shard_map/dot_general | solution.py:53
  192.1 3.0 fusion.111
  207.5 44.6 %attn_bwd.1 = (bf16[2,1024,128]{2,1,0:T(8,128)(2,1)}, bf16[2,4096,128]{2,1,0:T(8,128)(2,1)}, bf16[2,4096,128]{2,1,0:T(8,128)(2,1)}) custom-call(s32[2]{0:T(128)} %len_ref.3, bf16[2,2,1024,128]{3,2,1,0:T(8,128)(2,1)} %get-tuple-element.35.qa_ref, bf16[2,2,1024,128]{3,2,1,0:T(8,128)(2,1)} %pad_maximum_fusion.10.da_ref, ...), custom_call_target="tpu_custom_call" | custom-call | tf_op jit(solution)/shard_map/attn_bwd/pallas_call | solution.py:244
  257.3 5.5 %multiply_convert_fusion = bf16[2,1024,256]{2,1,0:T(8,128)(2,1)} fusion(f32[2,1024,256]{2,1,0:T(8,128)} %copy-done.2, bf16[2,1024,1024]{2,1,0:T(8,128)(2,1)} %get-tuple-element.89, f32[256]{0:T(256)S(1)} %bitcast.207, f32[2,1024]{1,0:T(2,128)S(1)} %get-tuple-element.136, bf16[1024,256]{1,0:T(8,128)(2,1)S(1)} %copy-done.39), kind=kOutput, calls=%fused_computation.78 | convolution fusion | flops 1075838976 | bytes 7873536 | tf_op jit(solution)/shard_map/dot_general | solution.py:53
  269.6 3.1 convolution_bitcast_fusion.6.refs_5_
  276.0 2.8 convolution_bitcast_fusion.refs_7_
  279.0 2.9 fusion.43.refs_6_
  287.5 30.6 %reduce-scatter.5.cloned.1.call-done = bf16[2,1024,128]{2,1,0:T(8,128)(2,1)} async-done(((bf16[2,4096,128]{2,1,0:T(8,128)(2,1)}), bf16[2,1024,128]{2,1,0:T(8,128)(2,1)}) %reduce-scatter.5.cloned.1.call-update) | async-done | bytes 524304 | tf_op jit(solution)/shard_map/reduce_scatter | solution.py:509
  328.0 4.2 multiply_reduce_fusion.5
  334.3 5.7 %all-reduce.3 = (f32[2,8]{1,0:T(2,128)S(1)}, f32[2,8]{1,0:T(2,128)S(1)}) all-reduce(f32[2,8]{1,0:T(2,128)S(1)} %reduce_sum.508, f32[2,8]{1,0:T(2,128)S(1)} %neg.47), channel_id=1, replica_groups=mesh['dp'=8,'seq'=4] {'seq'}, use_global_device_ids=true, to_apply=%region_28.30 | all-reduce | flops 32 | bytes 256 | tf_op jit(solution)/shard_map/psum | solution.py:120
  342.9 2.6 collective-permute-start.6
  345.5 3.5 collective-permute-start.7
  352.8 5.9 %multiply_reduce_fusion.6 = (f32[256]{0:T(256)S(1)}, f32[2,256]{1,0:T(2,128)S(1)}, f32[2,256]{1,0:T(2,128)S(1)}, f32[256]{0:T(256)S(1)}, f32[2,1024,256]{2,1,0:T...) fusion(f32[2,256]{1,0:T(2,128)S(1)} %copy-done.64, f32[2,256]{1,0:T(2,128)S(1)} %copy-done.56, ...), kind=kOutput, calls=%fused_computation.52 | convolution fusion | flops 839383296 | bytes 7757824 | tf_op jit(solution)/shard_map/dot_general | solution.py:53
  359.1 5.1 %all-reduce.2 = (f32[2,8]{1,0:T(2,128)S(1)}, f32[2,8]{1,0:T(2,128)S(1)}) all-reduce(f32[2,8]{1,0:T(2,128)S(1)} %reduce_sum.514, f32[2,8]{1,0:T(2,128)S(1)} %neg.48), channel_id=1, replica_groups=mesh['dp'=8,'seq'=4] {'seq'}, use_global_device_ids=true, to_apply=%region_34.36 | all-reduce | flops 32 | bytes 256 | tf_op jit(solution)/shard_map/psum | solution.py:120
  364.7 3.3 fusion.114
  368.9 3.2 multiply_reduce_fusion.7.refs_3_
  374.1 61.0 %reduce_weights.1 = (f32[768,256]{1,0:T(8,128)}, f32[768,256]{1,0:T(8,128)}, f32[256,256]{1,0:T(8,128)}, f32[1024,256]{1,0:T(8,128)}, f32[256,384]{1,0:T(8,128)}...) custom-call(f32[768,256]{1,0:T(8,128)} %convolution_bitcast_fusion.2, ...), custom_call_target="tpu_custom_call" | custom-call | tf_op jit(solution)/shard_map/reduce_weights/pallas_call | solution.py:372
  441.3 3.5 collective-permute-start.9
  446.0 4.7 %add_multiply_fusion = f32[2,1024,256]{2,1,0:T(8,128)} fusion(f32[2,1024,256]{2,1,0:T(8,128)S(1)} %copy-done.26, bf16[768,256,1]{1,0,2:T(8,128)(2,1)S(1)} %bitcast.160, bf16[2,1024,256]{2,1,0:T(8,128)(2,1)} %get-tuple-element.84, bf16[2,1,256]{2,1,0:T(2,128)(2,1)S(1)} %collective-permute-done.9, bf16[2,1,256]{2,1,0:T(2,128)(2,1)S(1)} %collective-permute-done.8, ...), kind=kOutput, calls=%fused_computation.54 | convolution fusion | flops 822083584 | bytes 5646336 | tf_op jit(solution)/shard_map/dot_general | solution.py:53
  (406 shorter events, 108.2 us)
Async XLA Ops:
  7.2 139.9 %copy-start = (bf16[256,1024]{1,0:T(8,128)(2,1)S(1)}, bf16[256,1024]{1,0:T(8,128)(2,1)}, u32[]{:S(2)}) copy-start(bf16[256,1024]{1,0:T(8,128)(2,1)} %param.28) | copy-start | bytes 1572868
  7.3 83.2 %all-gather.3.cloned.1.call-start = ((), (), s32[]{:S(2)}) async-start(), calls=%async_computation.2 | async-start | bytes 2621440 | tf_op jit(solution)/shard_map/all_gather | solution.py:437
  9.8 7.4 %collective-permute-start = (bf16[2,1,256]{2,1,0:T(2,128)(2,1)S(1)}, bf16[2,1,256]{2,1,0:T(2,128)(2,1)S(1)}, u32[]{:S(2)}, u32[]{:S(2)}) collective-permute-start(bf16[2,1,256]{2,1,0:T(2,128)(2,1)S(1)} %get-tuple-element.106), channel_id=1, source_target_pairs={{0,1},{1,2},{2,3},{4,5},{5,6},{6,7},{8,9},{9,10},{10,11},{12,13},{... | collective-permute-start | bytes 3080 | tf_op jit(solution)/shard_map/ppermute | solution.py:36
  14.3 4.9 %collective-permute-start.1 = (bf16[2,1,256]{2,1,0:T(2,128)(2,1)S(1)}, bf16[2,1,256]{2,1,0:T(2,128)(2,1)S(1)}, u32[]{:S(2)}, u32[]{:S(2)}) collective-permute-start(bf16[2,1,256]{2,1,0:T(2,128)(2,1)S(1)} %get-tuple-element.107), channel_id=1, source_target_pairs={{1,0},{2,1},{3,2},{5,4},{6,5},{7,6},{9,8},{10,9},{11,10},{13,12},{... | collective-permute-start | bytes 3080 | tf_op jit(solution)/shard_map/ppermute | solution.py:37
  16.9 16.5 %copy-start.69 = (f32[1,256]{1,0:T(1,128)}, f32[1,256]{1,0:T(1,128)S(1)}, u32[]{:S(2)}) copy-start(f32[1,256]{1,0:T(1,128)S(1)} %get-tuple-element.127) | copy-start | bytes 3076
  16.9 16.5 %copy-start.86 = (f32[1,256]{1,0:T(1,128)}, f32[1,256]{1,0:T(1,128)S(1)}, u32[]{:S(2)}) copy-start(f32[1,256]{1,0:T(1,128)S(1)} %get-tuple-element.126) | copy-start | bytes 3076
  16.9 41.6 %copy-start.71 = (f32[1,256]{1,0:T(1,128)}, f32[1,256]{1,0:T(1,128)S(1)}, u32[]{:S(2)}) copy-start(f32[1,256]{1,0:T(1,128)S(1)} %get-tuple-element.124) | copy-start | bytes 3076
  16.9 41.6 %copy-start.88 = (f32[1,256]{1,0:T(1,128)}, f32[1,256]{1,0:T(1,128)S(1)}, u32[]{:S(2)}) copy-start(f32[1,256]{1,0:T(1,128)S(1)} %get-tuple-element.123) | copy-start | bytes 3076
  16.9 46.4 %copy-start.90 = (f32[1,256]{1,0:T(1,128)}, f32[1,256]{1,0:T(1,128)S(1)}, u32[]{:S(2)}) copy-start(f32[1,256]{1,0:T(1,128)S(1)} %get-tuple-element.121) | copy-start | bytes 3076
  16.9 16.5 %copy-start.79 = (f32[1,256]{1,0:T(1,128)}, f32[1,256]{1,0:T(1,128)S(1)}, u32[]{:S(2)}) copy-start(f32[1,256]{1,0:T(1,128)S(1)} %get-tuple-element.139) | copy-start | bytes 3076
  16.9 41.6 %copy-start.81 = (f32[1,256]{1,0:T(1,128)}, f32[1,256]{1,0:T(1,128)S(1)}, u32[]{:S(2)}) copy-start(f32[1,256]{1,0:T(1,128)S(1)} %get-tuple-element.138) | copy-start | bytes 3076
  16.9 46.4 %copy-start.57 = (f32[1,256]{1,0:T(1,128)}, f32[1,256]{1,0:T(1,128)S(1)}, u32[]{:S(2)}) copy-start(f32[1,256]{1,0:T(1,128)S(1)} %get-tuple-element.140) | copy-start | bytes 3076
  16.9 173.2 %copy-start.59 = (f32[1,256]{1,0:T(1,128)}, f32[1,256]{1,0:T(1,128)S(1)}, u32[]{:S(2)}) copy-start(f32[1,256]{1,0:T(1,128)S(1)} %get-tuple-element.137) | copy-start | bytes 3076
  20.6 14.7 %copy-start.11 = (f32[2,1024,256]{2,1,0:T(8,128)}, f32[2,1024,256]{2,1,0:T(8,128)S(1)}, u32[]{:S(2)}) copy-start(f32[2,1024,256]{2,1,0:T(8,128)S(1)} %get-tuple-element.142) | copy-start | bytes 6291460
  26.5 17.6 %copy-start.41 = (bf16[3,256,256]{2,1,0:T(8,128)(2,1)S(1)}, bf16[3,256,256]{2,1,0:T(8,128)(2,1)}, u32[]{:S(2)}) copy-start(bf16[3,256,256]{2,1,0:T(8,128)(2,1)} %param.23) | copy-start | bytes 1179652
  35.3 5.8 %collective-permute-start.2 = (bf16[2,1,256]{2,1,0:T(2,128)(2,1)S(1)}, bf16[2,1,256]{2,1,0:T(2,128)(2,1)S(1)}, u32[]{:S(2)}, u32[]{:S(2)}) collective-permute-start(bf16[2,1,256]{2,1,0:T(2,128)(2,1)S(1)} %get-tuple-element.104), channel_id=1, source_target_pairs={{0,1},{1,2},{2,3},{4,5},{5,6},{6,7},{8,9},{9,10},{10,11},{12,13},{... | collective-permute-start | bytes 3080 | tf_op jit(solution)/shard_map/ppermute | solution.py:36
  39.2 4.9 %collective-permute-start.3 = (bf16[2,1,256]{2,1,0:T(2,128)(2,1)S(1)}, bf16[2,1,256]{2,1,0:T(2,128)(2,1)S(1)}, u32[]{:S(2)}, u32[]{:S(2)}) collective-permute-start(bf16[2,1,256]{2,1,0:T(2,128)(2,1)S(1)} %get-tuple-element.105), channel_id=1, source_target_pairs={{1,0},{2,1},{3,2},{5,4},{6,5},{7,6},{9,8},{10,9},{11,10},{13,12},{... | collective-permute-start | bytes 3080 | tf_op jit(solution)/shard_map/ppermute | solution.py:37
  65.8 49.3 %all-gather.5.cloned.1.call-start = ((), (), s32[]{:S(2)}) async-start(), calls=%async_computation.3 | async-start | bytes 2621440 | tf_op jit(solution)/shard_map/all_gather | solution.py:438
  66.6 219.0 %reduce-scatter.3.cloned.1.call-start = ((), (), s32[]{:S(2)}) async-start(), calls=%async_computation.4 | async-start | bytes 2621440 | tf_op jit(solution)/shard_map/reduce_scatter | solution.py:508
  68.5 5.2 %collective-permute-start.5 = (f32[2,1,256]{2,1,0:T(1,128)S(1)}, f32[2,1,256]{2,1,0:T(1,128)S(1)}, u32[]{:S(2)}, u32[]{:S(2)}) collective-permute-start(f32[2,1,256]{2,1,0:T(1,128)S(1)} %slice.253), channel_id=1, source_target_pairs={{1,0},{2,1},{3,2},{5,4},{6,5},{7,6},{9,8},{10,9},{11,10},{13,12},{... | collective-permute-start | bytes 6152 | tf_op jit(solution)/shard_map/ppermute | solution.py:45
  115.2 29.4 %copy-start.46 = (bf16[128,256]{1,0:T(8,128)(2,1)S(1)}, bf16[128,256]{1,0:T(8,128)(2,1)}, u32[]{:S(2)}) copy-start(bf16[128,256]{1,0:T(8,128)(2,1)} %param.27) | copy-start | bytes 196612
  115.2 29.4 %copy-start.92 = (f32[1,256]{1,0:T(1,128)S(1)}, f32[1,256]{1,0:T(1,128)}, u32[]{:S(2)}) copy-start(f32[1,256]{1,0:T(1,128)} %get-tuple-element.120) | copy-start | bytes 3076
  146.4 45.7 %copy-start.2 = (f32[2,1024,256]{2,1,0:T(8,128)}, f32[2,1024,256]{2,1,0:T(8,128)S(1)}, u32[]{:S(2)}) copy-start(f32[2,1024,256]{2,1,0:T(8,128)S(1)} %get-tuple-element.148) | copy-start | bytes 6291460
  252.1 66.0 %reduce-scatter.5.cloned.1.call-start = ((), (), s32[]{:S(2)}) async-start(), calls=%async_computation.5 | async-start | bytes 2621440 | tf_op jit(solution)/shard_map/reduce_scatter | solution.py:509
  265.9 16.6 %collective-permute-start.4 = (bf16[2,1,256]{2,1,0:T(2,128)(2,1)S(1)}, bf16[2,1,256]{2,1,0:T(2,128)(2,1)S(1)}, u32[]{:S(2)}, u32[]{:S(2)}) collective-permute-start(bf16[2,1,256]{2,1,0:T(2,128)(2,1)S(1)} %slice.246), channel_id=1, source_target_pairs={{0,1},{1,2},{2,3},{4,5},{5,6},{6,7},{8,9},{9,10},{10,11},{12,13},{... | collective-permute-start | bytes 3080 | tf_op jit(solution)/shard_map/ppermute | solution.py:45
  285.6 34.4 %copy-start.58 = (f32[1,256]{1,0:T(1,128)S(1)}, f32[1,256]{1,0:T(1,128)}, u32[]{:S(2)}) copy-start(f32[1,256]{1,0:T(1,128)} %copy-done.57) | copy-start | bytes 3076
  342.9 9.4 %collective-permute-start.6 = (bf16[2,1,256]{2,1,0:T(2,128)(2,1)S(1)}, bf16[2,1,256]{2,1,0:T(2,128)(2,1)S(1)}, u32[]{:S(2)}, u32[]{:S(2)}) collective-permute-start(bf16[2,1,256]{2,1,0:T(2,128)(2,1)S(1)} %get-tuple-element.100), channel_id=1, source_target_pairs={{1,0},{2,1},{3,2},{5,4},{6,5},{7,6},{9,8},{10,9},{11,10},{13,12},{... | collective-permute-start | bytes 3080 | tf_op jit(solution)/shard_map/ppermute | solution.py:37
  345.5 6.8 %collective-permute-start.7 = (bf16[2,1,256]{2,1,0:T(2,128)(2,1)S(1)}, bf16[2,1,256]{2,1,0:T(2,128)(2,1)S(1)}, u32[]{:S(2)}, u32[]{:S(2)}) collective-permute-start(bf16[2,1,256]{2,1,0:T(2,128)(2,1)S(1)} %get-tuple-element.101), channel_id=1, source_target_pairs={{0,1},{1,2},{2,3},{4,5},{5,6},{6,7},{8,9},{9,10},{10,11},{12,13},{... | collective-permute-start | bytes 3080 | tf_op jit(solution)/shard_map/ppermute | solution.py:36
  374.1 71.9 %copy-start.26 = (f32[2,1024,256]{2,1,0:T(8,128)S(1)}, f32[2,1024,256]{2,1,0:T(8,128)}, u32[]{:S(2)}) copy-start(f32[2,1024,256]{2,1,0:T(8,128)} %fusion.65) | copy-start | bytes 6291460
  374.1 71.9 %copy-start.43 = (bf16[3,256,256]{1,2,0:T(8,128)(2,1)S(1)}, bf16[3,256,256]{1,2,0:T(8,128)(2,1)}, u32[]{:S(2)}) copy-start(bf16[3,256,256]{1,2,0:T(8,128)(2,1)} %copy.90) | copy-start | bytes 1179652
  439.2 6.8 %collective-permute-start.8 = (bf16[2,1,256]{2,1,0:T(2,128)(2,1)S(1)}, bf16[2,1,256]{2,1,0:T(2,128)(2,1)S(1)}, u32[]{:S(2)}, u32[]{:S(2)}) collective-permute-start(bf16[2,1,256]{2,1,0:T(2,128)(2,1)S(1)} %get-tuple-element.98), channel_id=1, source_target_pairs={{1,0},{2,1},{3,2},{5,4},{6,5},{7,6},{9,8},{10,9},{11,10},{13,12},{... | collective-permute-start | bytes 3080 | tf_op jit(solution)/shard_map/ppermute | solution.py:37
  441.3 4.7 %collective-permute-start.9 = (bf16[2,1,256]{2,1,0:T(2,128)(2,1)S(1)}, bf16[2,1,256]{2,1,0:T(2,128)(2,1)S(1)}, u32[]{:S(2)}, u32[]{:S(2)}) collective-permute-start(bf16[2,1,256]{2,1,0:T(2,128)(2,1)S(1)} %get-tuple-element.99), channel_id=1, source_target_pairs={{0,1},{1,2},{2,3},{4,5},{5,6},{6,7},{8,9},{9,10},{10,11},{12,13},{... | collective-permute-start | bytes 3080 | tf_op jit(solution)/shard_map/ppermute | solution.py:36
  (96 other events, 430.4 us)
Sparse Core Ops, SparseCore 0:
  66.0 24.4 all-gather.2
  92.6 22.5 all-gather.4
  252.2 31.8 reduce-scatter.2
  286.7 31.4 reduce-scatter.4

commit v3 on v2

--- a/solution.py
+++ b/solution.py
@@ -11,6 +11,7 @@
 F32, BF = jnp.float32, jnp.bfloat16
 NT = (((1,), (1,)), ((), ()))
 NN = (((1,), (0,)), ((), ()))
+TN = (((0,), (0,)), ((), ()))
 LOG2E = math.log2(math.e)
 MESH = pl.DeviceIdType.MESH
 
@@ -135,130 +136,232 @@
     return centered * lax.rsqrt(variance + norm_eps) * gain + shift
 
 
-def snake(values, snake_logs):
-    return values + jnp.square(jnp.sin(values * jnp.exp(snake_logs[0]))) / (
-        jnp.exp(snake_logs[1]) + 1e-09
-    )
-
-
-def fwd_kernel(QB, CK, len_ref, q_ref, k_ref, v_ref, o_ref, qa_ref, kb, vb):
-    u = pl.program_id(0)
-    W = k_ref.shape[1]; F = q_ref.shape[1]
-    L = len_ref[u]
+SIN_PI = (3.141592580060032, -5.167706879868365, 2.55003139258664, -0.598045264752551, 0.0772203056339658)
+COS_PI = (0.9999999534804945, -4.934792860766467, 4.05841196261883, -1.3318805129033002, 0.21969758323424166)
+
+
+def horner(coefficients, x):
+    value = coefficients[-1]
+    for coefficient in coefficients[-2::-1]:
+        value = value * x + coefficient
+    return value
+
+
+def sin_cos_half_turns(turns):
+    part = turns - jnp.round(turns)
+    square = part * part
+    return part * horner(SIN_PI, square), horner(COS_PI, square)
+
+
+def row_sum(x):
+    return jnp.sum(x, axis=0, keepdims=True)
+
+
+def lane_mean(x):
+    return jnp.mean(x, axis=1, keepdims=True)
+
+
+def tn(a, b):
+    return lax.dot_general(a, b, TN, preferred_element_type=F32)
+
+
+def middle_kernel(
+    RB,
+    FC,
+    len_ref,
+    att_ref,
+    res_ref,
+    cot_ref,
+    next_ref,
+    w_out,
+    ff_in,
+    ff_out,
+    conv_down,
+    gains,
+    shifts,
+    ff_bias,
+    snake_logs,
+    out_ref,
+    gtwo_ref,
+    aug_ref,
+    last_ref,
+    gw_out,
+    gff_in,
+    gff_out,
+    gdown,
+    gsmall,
+    gff_small,
+    pairs,
+    before_last,
+    acc_out,
+):
+    u, i = pl.program_id(0), pl.program_id(1)
+    U, nb = pl.num_programs(0), pl.num_programs(1)
+    half = RB // 2
+    frames = nb * RB
+    length = len_ref[u]
+    base = lax.axis_index("seq") * frames
+    at = base + i * RB
+
+    @pl.when((u == 0) & (i == 0))
+    def _():
+        for ref in (gw_out, gff_in, gdown, gsmall, gff_small, acc_out):
+            ref[...] = jnp.zeros_like(ref)
+
+    def column_mask(start, rows, step):
+        places = start + step * lax.broadcasted_iota(jnp.int32, (rows, 1), 0)
+        return jnp.where(places < length, 1.0, 0.0)
+
+    mask = column_mask(at, RB, 1)
+    half_mask = column_mask(at, half, 2)
+    low_f32 = cot_ref[0, pl.ds(pl.multiple_of(i * half, half), half), :].astype(F32) * half_mask
+    gsmall[4:5, :] += row_sum(low_f32)
+    low = low_f32.astype(BF)
+    follow = jnp.minimum(i * half + half, frames // 2 - 16)
+    inner = cot_ref[0, pl.ds(pl.multiple_of(follow, 16), 16), :].astype(F32)[0:1]
+    outer = next_ref[0].astype(F32)[0:1]
+    after = jnp.where(i == nb - 1, outer, inner) * jnp.where(at + RB < length, 1.0, 0.0)
+    row_at = lax.broadcasted_iota(jnp.int32, (half, 1), 0)
+    low_next = jnp.where(row_at == half - 1, after, pltpu.roll(low_f32, half - 1, 0)).astype(BF)
+    even_grads = dot(low, conv_down[1], NT)
+    odd_grads = dot(low, conv_down[2], NT) + dot(low_next, conv_down[0], NT)
+    for lanes in (0, 128):
+        pairs[lanes // 128, pl.ds(0, half, stride=2), :] = even_grads[:, lanes : lanes + 128]
+        pairs[lanes // 128, pl.ds(1, half, stride=2), :] = odd_grads[:, lanes : lanes + 128]
+    grad_three = jnp.concatenate([pairs[0], pairs[1]], axis=1) * mask
+    gsmall[3:4, :] += row_sum(grad_three)
+    grad_low = grad_three.astype(BF)
+    attended = att_ref[0]
+    att_low = attended.astype(BF)
+    resid_two = res_ref[0] + dot(att_low, w_out[...]) + shifts[7:8, :]
+    centered = resid_two - lane_mean(resid_two)
+    inv = lax.rsqrt(lane_mean(centered * centered) + norm_eps)
+    hat = centered * inv
+    normed = (hat * gains[3:4, :] + shifts[8:9, :]).astype(BF)
+    freq = jnp.exp(snake_logs[0:1, :])
+    spread = jnp.exp(snake_logs[1:2, :])
+    size = 1.0 / (spread + 1e-09)
+    turn = freq * (1.0 / math.pi)
+    resid_three = resid_two + shifts[9:10, :]
+    grad_normed = jnp.zeros_like(resid_two)
+    for c in range(0, ff_bias.shape[1], FC):
+        cols = slice(c, c + FC)
+        hidden = dot(normed, ff_in[:, cols]) + ff_bias[:, cols]
+        sine, cosine = sin_cos_half_turns(hidden * turn[:, cols])
+        square = sine * sine
+        snaked = (hidden + square * size[:, cols]).astype(BF)
+        resid_three = resid_three + dot(snaked, ff_out[cols, :])
+        acc_out[:, cols] += tn(grad_low, snaked)
+        grad_snaked = dot(grad_low, ff_out[cols, :], NT)
+        cross = grad_snaked * (sine * cosine)
+        grad_hidden = grad_snaked + cross * (2.0 * size * freq)[:, cols]
+        gff_small[0:1, cols] += row_sum(grad_hidden)
+        gff_small[1:2, cols] += row_sum(cross * hidden)
+        gff_small[2:3, cols] += row_sum(grad_snaked * square)
+        hidden_low = grad_hidden.astype(BF)
+        gff_in[:, cols] += tn(normed, hidden_low)
+        grad_normed = grad_normed + dot(hidden_low, ff_in[:, cols], NT)
+    down = (resid_three * mask).astype(BF)
+    down_f32 = down.astype(F32)
+    for lanes in (0, 128):
+        pairs[lanes // 128] = down_f32[:, lanes : lanes + 128]
+    even = jnp.concatenate([pairs[j, pl.ds(0, half, stride=2), :] for j in range(2)], axis=1)
+    odd = jnp.concatenate([pairs[j, pl.ds(1, half, stride=2), :] for j in range(2)], axis=1)
+    first = jnp.where(i == 0, 0.0, before_last[0:1, :])
+    before = jnp.where(row_at == 0, first, pltpu.roll(odd, 1, 0)).astype(BF)
+    before_last[0:1, :] = odd[half - 1 : half, :]
+    last_ref[0] = down[RB - 16 :, :]
+    even, odd = even.astype(BF), odd.astype(BF)
+    lowered = dot(before, conv_down[0]) + dot(even, conv_down[1]) + dot(odd, conv_down[2])
+    out_ref[0] = ((lowered + shifts[10:11, :]) * half_mask).astype(BF)
+    gdown[0] += tn(before, low)
+    gdown[1] += tn(even, low)
+    gdown[2] += tn(odd, low)
+    gsmall[0:1, :] += row_sum(grad_normed * hat)
+    gsmall[2:3, :] += row_sum(grad_normed)
+    grad_hat = grad_normed * gains[3:4, :]
+    grad_two = grad_three + inv * (
+        grad_hat - lane_mean(grad_hat) - hat * lane_mean(grad_hat * hat)
+    )
+    gtwo_ref[0] = grad_two
+    gsmall[1:2, :] += row_sum(grad_two)
+    two_low = grad_two.astype(BF)
+    gw_out[...] += tn(att_low, two_low)
+    grad_att = dot(two_low, w_out[...], NT).astype(BF)
+    terms = grad_att.astype(F32) * attended
     lane = lax.broadcasted_iota(jnp.int32, (1, 128), 1)
-    first = lane < 64
-    c = 0.125 * LOG2E
-    nch = (L + CK - 1) // CK
-    one = jnp.ones((), BF)
-    for qi in range(F // QB):
-        q = q_ref[0, qi * QB:(qi + 1) * QB, :]
-        qh = [jnp.where(first, q, jnp.zeros_like(q)), jnp.where(first, jnp.zeros_like(q), q)]
-        def body(j, carry):
-            off = pl.multiple_of(j * CK, CK)
-            k = k_ref[0, pl.ds(off, CK), :]
-            v = v_ref[0, pl.ds(off, CK), :]
-            vh = [jnp.where(first, v, one), jnp.where(first, one, v)]
-            bias = jnp.where(off + lax.broadcasted_iota(jnp.int32, (1, CK), 1) < L, 0.0, -1e9)
-            out = []
-            for h in range(2):
-                m, acc = carry[h]
-                s = dot(qh[h], k, NT) + bias
-                mn = jnp.maximum(m, jnp.max(s, axis=1, keepdims=True))
-                p = jnp.exp2((s - mn) * c).astype(BF)
-                al = jnp.exp2((m - mn) * c)
-                acc = acc * al + dot(p, vh[h])
-                out.append((mn, acc))
-            return tuple(out)
-        init = tuple((jnp.full((QB, 1), -1e30, F32), jnp.zeros((QB, 128), F32)) for _ in range(2))
-        (m0, a0), (m1, a1) = lax.fori_loop(0, nch, body, init)
-        l0 = a0[:, 64:65]; l1 = a1[:, 0:1]
-        o_ref[0, qi * QB:(qi + 1) * QB, :] = jnp.where(first, a0 / l0, a1 / l1)
-        for h, (m, l) in enumerate(((m0, l0), (m1, l1))):
-            t = -(m + jnp.log2(l) / c)
-            t1 = t.astype(BF); r = t - t1.astype(F32); t2 = r.astype(BF); r = r - t2.astype(F32); t3 = r.astype(BF)
-            base = 64 * (1 - h)
-            qa = jnp.where(lane == base, t1, jnp.where(lane == base + 1, t2, jnp.where(lane == base + 2, t3,
-                 jnp.where(lane == base + 3, one, qh[h]))))
-            qa_ref[0, h, qi * QB:(qi + 1) * QB, :] = qa
-
-def attn_forward(lengths, q, k, v, QB=1024, CK=2048):
-    U, F, _ = q.shape; W = k.shape[1]
+    zero = jnp.zeros((), F32)
+    for h in range(2):
+        mine = (lane >= 64 * h) & (lane < 64 * h + 64)
+        term = jnp.sum(jnp.where(mine, terms, zero), axis=1, keepdims=True)
+        aug_ref[0, h] = with_pieces(jnp.where(mine, grad_att, jnp.zeros((), BF)), term, lane, h)
+
+    @pl.when((u == U - 1) & (i == nb - 1))
+    def _():
+        gff_out[...] = acc_out[...].T
+        gff_small[1:2, :] = gff_small[1:2, :] * (2.0 * size * freq)
+        gff_small[2:3, :] = gff_small[2:3, :] * (-(size * size) * spread)
+
+
+def with_pieces(block, value, lane, h):
+    base = 64 * (1 - h)
+    for j in range(3):
+        piece = value.astype(BF)
+        value = value - piece.astype(F32)
+        block = jnp.where(lane == base + j, piece, block)
+    return block
+
+
+def middle(lengths, attended, resnet_out, cotangent, next_rows, w_out, ff_in, ff_out, conv_down, gains, shifts, ff_bias, snake_logs, RB=512, FC=256):
+    U, F, C = resnet_out.shape
+    inner = attended.shape[2]
+    FF = ff_bias.shape[0]
+    whole = lambda shape: pl.BlockSpec(shape, lambda u, i, _: (0,) * len(shape))
+    rows = lambda n, c: pl.BlockSpec((1, n, c), lambda u, i, _: (u, i, 0))
+    per_utt = lambda n, c: pl.BlockSpec((1, n, c), lambda u, i, _: (u, 0, 0))
+    sums = ((inner, C), (C, FF), (FF, C), (3, C, C), (8, C), (8, FF))
     return pl.pallas_call(
-        functools.partial(fwd_kernel, QB, CK),
-        out_shape=(jax.ShapeDtypeStruct((U, F, 128), F32), jax.ShapeDtypeStruct((U, 2, F, 128), BF)),
-        grid_spec=pltpu.PrefetchScalarGridSpec(num_scalar_prefetch=1, grid=(U,),
-            in_specs=[pl.BlockSpec((1, F, 128), lambda u, _: (u, 0, 0)), pl.BlockSpec((1, W, 128), lambda u, _: (u, 0, 0)), pl.BlockSpec((1, W, 128), lambda u, _: (u, 0, 0))],
-            out_specs=[pl.BlockSpec((1, F, 128), lambda u, _: (u, 0, 0)), pl.BlockSpec((1, 2, F, 128), lambda u, _: (u, 0, 0, 0))],
-            scratch_shapes=[pltpu.VMEM((2, W, 128), BF), pltpu.VMEM((2, W, 128), BF)]),
-        compiler_params=pltpu.CompilerParams(vmem_limit_bytes=56 * 2**20), name="attn_fwd",
-    )(lengths, q, k, v)
-
-def bwd_kernel(KB, len_ref, qa_ref, da_ref, k_ref, v_ref, dq_ref, dk_ref, dv_ref, dqt):
-    u = pl.program_id(0)
-    W = k_ref.shape[1]; F = qa_ref.shape[2]
-    L = len_ref[u]
-    lane = lax.broadcasted_iota(jnp.int32, (1, 128), 1)
-    first = lane < 64
-    c = 0.125 * LOG2E
-    one = jnp.ones((), BF)
-    dqt[...] = jnp.zeros_like(dqt)
-    nkb = (L + KB - 1) // KB
-    def body(j, _):
-        off = pl.multiple_of(j * KB, KB)
-        k = k_ref[0, pl.ds(off, KB), :]
-        v = v_ref[0, pl.ds(off, KB), :]
-        kt = k.T
-        bias = jnp.where(off + lax.broadcasted_iota(jnp.int32, (KB, 1), 0) < L, 0.0, -1e9).astype(BF)
-        dvs, dks = [], []
-        for h in range(2):
-            base = 64 * (1 - h)
-            if h == 0:
-                ka = jnp.where(lane < 64, k, jnp.where(lane == base + 3, bias, jnp.where(lane < base + 3, one, 0 * one)))
-                va = jnp.where(lane < 64, v, jnp.where(lane < base + 3, -one, 0 * one))
-            else:
-                ka = jnp.where(lane >= 64, k, jnp.where(lane == base + 3, bias, jnp.where(lane < base + 3, one, 0 * one)))
-                va = jnp.where(lane >= 64, v, jnp.where(lane < base + 3, -one, 0 * one))
-            qa = qa_ref[0, h]
-            da = da_ref[0, h]
-            st = dot(ka, qa, NT)
-            p = jnp.exp2(st * c)
-            dp = dot(va, da, NT)
-            ds = (p * dp).astype(BF)
-            dvs.append(dot(p.astype(BF), da))
-            dks.append(dot(ds, qa))
-            dqt[h * 64:(h + 1) * 64, :] += dot(kt[h * 64:(h + 1) * 64, :], ds)
-        dk_ref[0, pl.ds(off, KB), :] = (jnp.where(first, dks[0], dks[1]) * 0.125).astype(BF)
-        dv_ref[0, pl.ds(off, KB), :] = jnp.where(first, dvs[0], dvs[1]).astype(BF)
-        return 0
-    lax.fori_loop(0, nkb, body, 0)
-    def zero(j, _):
-        off = pl.multiple_of(j * KB, KB)
-        dk_ref[0, pl.ds(off, KB), :] = jnp.zeros((KB, 128), BF)
-        dv_ref[0, pl.ds(off, KB), :] = jnp.zeros((KB, 128), BF)
-        return 0
-    lax.fori_loop(nkb, W // KB, zero, 0)
-    dq_ref[0] = (dqt[...] * 0.125).T.astype(BF)
-
-def attn_backward(lengths, qa, da, k, v, KB=512):
-    U, _, F, _ = qa.shape; W = k.shape[1]
-    return pl.pallas_call(
-        functools.partial(bwd_kernel, KB),
-        out_shape=(jax.ShapeDtypeStruct((U, F, 128), BF), jax.ShapeDtypeStruct((U, W, 128), BF), jax.ShapeDtypeStruct((U, W, 128), BF)),
-        grid_spec=pltpu.PrefetchScalarGridSpec(num_scalar_prefetch=1, grid=(U,),
-            in_specs=[pl.BlockSpec((1, 2, F, 128), lambda u, _: (u, 0, 0, 0)), pl.BlockSpec((1, 2, F, 128), lambda u, _: (u, 0, 0, 0)),
-                      pl.BlockSpec((1, W, 128), lambda u, _: (u, 0, 0)), pl.BlockSpec((1, W, 128), lambda u, _: (u, 0, 0))],
-            out_specs=[pl.BlockSpec((1, F, 128), lambda u, _: (u, 0, 0)), pl.BlockSpec((1, W, 128), lambda u, _: (u, 0, 0)), pl.BlockSpec((1, W, 128), lambda u, _: (u, 0, 0))],
-            scratch_shapes=[pltpu.VMEM((128, F), F32)]),
-        compiler_params=pltpu.CompilerParams(vmem_limit_bytes=56 * 2**20), name="attn_bwd",
-    )(lengths, qa, da, k, v)
-
-
-def split_bf16(t):
-    t1 = t.astype(BF)
-    r = t - t1.astype(F32)
-    t2 = r.astype(BF)
-    t3 = (r - t2.astype(F32)).astype(BF)
-    return jnp.stack([t1, t2, t3], axis=-1)
+        functools.partial(middle_kernel, RB, FC),
+        out_shape=(
+            jax.ShapeDtypeStruct((U, F // 2, C), BF),
+            jax.ShapeDtypeStruct((U, F, C), F32),
+            jax.ShapeDtypeStruct((U, 2, F, inner), BF),
+            jax.ShapeDtypeStruct((U, 16, C), BF),
+            *(jax.ShapeDtypeStruct(shape, F32) for shape in sums),
+        ),
+        grid_spec=pltpu.PrefetchScalarGridSpec(
+            num_scalar_prefetch=1,
+            grid=(U, F // RB),
+            in_specs=[
+                rows(RB, inner),
+                rows(RB, C),
+                per_utt(F // 2, C),
+                per_utt(16, C),
+                whole((inner, C)),
+                whole((C, FF)),
+                whole((FF, C)),
+                whole((3, C, C)),
+                whole(gains.shape),
+                whole(shifts.shape),
+                whole((1, FF)),
+                whole((2, FF)),
+            ],
+            out_specs=[
+                rows(RB // 2, C),
+                rows(RB, C),
+                pl.BlockSpec((1, 2, RB, inner), lambda u, i, _: (u, 0, i, 0)),
+                per_utt(16, C),
+                *(whole(shape) for shape in sums),
+            ],
+            scratch_shapes=[
+                pltpu.VMEM((2, RB, 128), F32),
+                pltpu.VMEM((8, C), F32),
+                pltpu.VMEM((C, FF), F32),
+            ],
+        ),
+        compiler_params=pltpu.CompilerParams(vmem_limit_bytes=56 * 2**20),
+        name="middle",
+    )(lengths, attended, resnet_out, cotangent, next_rows, w_out, ff_in, ff_out, conv_down, gains, shifts, ff_bias.reshape(1, -1), snake_logs)
 
 
 def butterfly(axes):
@@ -391,6 +494,251 @@
     return out[:-1], out[-1]
 
 
+SCALE2 = 0.125 * LOG2E
+
+
+def head_lanes(lane, h):
+    return (lane >= 64 * h) & (lane < 64 * h + 64)
+
+
+def greet_seq(me):
+    barrier = pltpu.get_barrier_semaphore()
+    for flip in (1, 2):
+        pl.semaphore_signal(barrier, inc=1, device_id={"seq": flipped(me, flip)}, device_id_type=MESH)
+    pl.semaphore_wait(barrier, 2)
+
+
+def flipped(place, bit):
+    return place + bit - 2 * bit * ((place // bit) % 2)
+
+
+def to_peer(src, dst, sems, place, peer):
+    return pltpu.make_async_remote_copy(
+        src, dst, sems.at[(0, *place)], sems.at[(1, *place)], device_id={"seq": peer}, device_id_type=MESH
+    )
+
+
+def forward_kernel(len_ref, q_ref, kv_ref, o_ref, qa_ref, all_ref, top, acc, sems):
+    U, F, _ = q_ref.shape
+    me = lax.axis_index("seq")
+    near, far = flipped(me, 1), flipped(me, 2)
+    lane = lax.broadcasted_iota(jnp.int32, (1, 128), 1)
+    one, zero = jnp.ones((), BF), jnp.zeros((), BF)
+    greet_seq(me)
+
+    def hop(kind, u):
+        if kind == 0:
+            return to_peer(kv_ref.at[u], all_ref.at[1, u], sems, (kind, u), near)
+        if kind == 1:
+            return to_peer(kv_ref.at[u], all_ref.at[2, u], sems, (kind, u), far)
+        return to_peer(all_ref.at[2, u], all_ref.at[3, u], sems, (kind, u), near)
+
+    hop(1, 0).start()
+    hop(0, 0).start()
+    hop(0, 1).start()
+    all_ref[0] = kv_ref[...]
+    top[...] = jnp.full(top.shape, -1e30, F32)
+    acc[...] = jnp.zeros(acc.shape, F32)
+
+    def step(i, _):
+        late = i // 4
+        r = (1 - late) * (i // 2) + late * (2 + i % 2)
+        u = (1 - late) * (i % 2) + late * ((i - 4) // 2)
+
+        @pl.when(i == 2)
+        def _():
+            hop(0, 0).wait_recv()
+
+        @pl.when(i == 3)
+        def _():
+            hop(1, 0).wait_send()
+            hop(1, 1).start()
+            hop(0, 1).wait_recv()
+
+        @pl.when(i == 4)
+        def _():
+            hop(1, 0).wait_recv()
+            hop(2, 0).start()
+
+        @pl.when(i == 5)
+        def _():
+            hop(2, 0).wait_recv()
+
+        @pl.when(i == 6)
+        def _():
+            hop(1, 1).wait_recv()
+            hop(2, 1).start()
+
+        @pl.when(i == 7)
+        def _():
+            hop(2, 1).wait_recv()
+
+        block = xor4(me, r)
+        spot = block * F + lax.broadcasted_iota(jnp.int32, (1, F), 1)
+        bias = jnp.where(spot < len_ref[u], 0.0, -1e9)
+        q = q_ref[u]
+        k = all_ref[r, u, :, 0:128]
+        v = all_ref[r, u, :, 128:256]
+        for h in range(2):
+            mine = head_lanes(lane, h)
+            s = dot(jnp.where(mine, q, zero), k, NT) + bias
+            old = top[u, h, :, 0:1]
+            new = jnp.maximum(old, jnp.max(s, axis=1, keepdims=True))
+            p = jnp.exp2((s - new) * SCALE2).astype(BF)
+            acc[u, h] = acc[u, h] * jnp.exp2((old - new) * SCALE2) + dot(p, jnp.where(mine, v, one))
+            top[u, h, :, 0:1] = new
+        return 0
+
+    lax.fori_loop(0, 8, step, 0)
+    for u in range(U):
+        outs = []
+        for h in range(2):
+            mine = head_lanes(lane, h)
+            sums = acc[u, h]
+            total = sums[:, 64 * (1 - h) : 64 * (1 - h) + 1]
+            outs.append(sums / total)
+            log_total = top[u, h, :, 0:1] + jnp.log2(total) / SCALE2
+            aug = jnp.where(mine, q_ref[u], jnp.where(lane == 64 * (1 - h) + 3, one, zero))
+            qa_ref[u, h] = with_pieces(aug, -log_total, lane, h)
+        o_ref[u] = jnp.where(head_lanes(lane, 0), outs[0], outs[1])
+    for u in range(U):
+        hop(0, u).wait_send()
+        hop(2, u).wait_send()
+    hop(1, 1).wait_send()
+
+
+def xor4(place, r):
+    low = (place % 2 + r % 2) % 2
+    high = (place // 2 + r // 2) % 2
+    return 2 * high + low
+
+
+def attend(lengths, q, kv):
+    U, F, _ = q.shape
+    vmem = pl.BlockSpec(memory_space=pltpu.VMEM)
+    return pl.pallas_call(
+        forward_kernel,
+        out_shape=(
+            jax.ShapeDtypeStruct((U, F, 128), F32),
+            jax.ShapeDtypeStruct((U, 2, F, 128), BF),
+            jax.ShapeDtypeStruct((4, U, F, 256), BF),
+        ),
+        in_specs=[pl.BlockSpec(memory_space=pltpu.SMEM), vmem, vmem],
+        out_specs=[vmem] * 3,
+        scratch_shapes=[
+            pltpu.VMEM((U, 2, F, 128), F32),
+            pltpu.VMEM((U, 2, F, 128), F32),
+            pltpu.SemaphoreType.DMA((2, 3, U)),
+        ],
+        compiler_params=pltpu.CompilerParams(
+            collective_id=1, has_side_effects=True, vmem_limit_bytes=56 * 2**20
+        ),
+        name="attend",
+    )(lengths, q, kv)
+
+
+def backward_kernel(KB, len_ref, qa_ref, da_ref, all_ref, grad_ref, dqt, part, sent, got, sems):
+    U, _, F, _ = qa_ref.shape
+    me = lax.axis_index("seq")
+    near, far = flipped(me, 1), flipped(me, 2)
+    lane = lax.broadcasted_iota(jnp.int32, (1, 128), 1)
+    one, zero = jnp.ones((), BF), jnp.zeros((), BF)
+    greet_seq(me)
+    dqt[...] = jnp.zeros(dqt.shape, F32)
+
+    def hop(kind, u):
+        peer = far if kind == 1 else near
+        return to_peer(sent.at[kind, u], got.at[kind, u], sems, (kind, u), peer)
+
+    def step(i, _):
+        late = i // 4
+        r = (1 - late) * (3 - i % 2) + late * (1 - (i - 4) // 2)
+        u = (1 - late) * ((i // 2) % 2) + late * (i % 2)
+        block = xor4(me, r)
+
+        def tile(j, _):
+            off = pl.multiple_of(j * KB, KB)
+            here = pl.ds(off, KB)
+            k = all_ref[r, u, here, 0:128]
+            v = all_ref[r, u, here, 128:256]
+            kt = k.T
+            spot = block * F + off + lax.broadcasted_iota(jnp.int32, (KB, 1), 0)
+            bias = jnp.where(spot < len_ref[u], 0.0, -1e9).astype(BF)
+            dks, dvs = [], []
+            for h in range(2):
+                mine = head_lanes(lane, h)
+                base = 64 * (1 - h)
+                extra = (lane >= base) & (lane < base + 3)
+                ka = jnp.where(mine, k, jnp.where(extra, one, jnp.where(lane == base + 3, bias, zero)))
+                va = jnp.where(mine, v, jnp.where(extra, -one, zero))
+                qa = qa_ref[u, h]
+                da = da_ref[u, h]
+                p = jnp.exp2(dot(ka, qa, NT) * SCALE2)
+                ds = (p * dot(va, da, NT)).astype(BF)
+                dvs.append(dot(p.astype(BF), da))
+                dks.append(dot(ds, qa))
+                rows = slice(64 * h, 64 * h + 64)
+                dqt[u, rows, :] += dot(kt[rows, :], ds)
+            part[here, 0:128] = jnp.where(head_lanes(lane, 0), dks[0], dks[1]) * 0.125
+            part[here, 128:256] = jnp.where(head_lanes(lane, 0), dvs[0], dvs[1])
+            return 0
+
+        lax.fori_loop(0, F // KB, tile, 0)
+
+        @pl.when(r == 3)
+        def _():
+            sent[0, u] = part[...].astype(BF)
+            hop(0, u).start()
+
+        @pl.when(r == 2)
+        def _():
+            hop(0, u).wait_recv()
+            sent[1, u] = (part[...] + got[0, u].astype(F32)).astype(BF)
+            hop(1, u).start()
+
+        @pl.when(r == 1)
+        def _():
+            sent[2, u] = part[...].astype(BF)
+            hop(2, u).start()
+
+        @pl.when(r == 0)
+        def _():
+            hop(1, u).wait_recv()
+            hop(2, u).wait_recv()
+            whole = part[...] + got[1, u].astype(F32) + got[2, u].astype(F32)
+            grad_ref[u, :, 128:384] = whole.astype(BF)
+            grad_ref[u, :, 0:128] = (dqt[u] * 0.125).T.astype(BF)
+
+        return 0
+
+    lax.fori_loop(0, 8, step, 0)
+    for kind in range(3):
+        for u in range(U):
+            hop(kind, u).wait_send()
+
+
+def attend_back(lengths, qa, da, kv_all, KB=512):
+    U, _, F, _ = qa.shape
+    vmem = pl.BlockSpec(memory_space=pltpu.VMEM)
+    return pl.pallas_call(
+        functools.partial(backward_kernel, KB),
+        out_shape=jax.ShapeDtypeStruct((U, F, 384), BF),
+        in_specs=[pl.BlockSpec(memory_space=pltpu.SMEM), vmem, vmem, vmem],
+        out_specs=vmem,
+        scratch_shapes=[
+            pltpu.VMEM((U, 128, F), F32),
+            pltpu.VMEM((F, 256), F32),
+            pltpu.VMEM((3, U, F, 256), BF),
+            pltpu.VMEM((3, U, F, 256), BF),
+            pltpu.SemaphoreType.DMA((2, 3, U)),
+        ],
+        compiler_params=pltpu.CompilerParams(
+            collective_id=2, has_side_effects=True, vmem_limit_bytes=56 * 2**20
+        ),
+        name="attend_back",
+    )(lengths, qa, da, kv_all)
+
+
 def shards(
     frames,
     time_embed,
@@ -412,7 +760,6 @@
 ):
     utt_count, frame_count, channels = frames.shape
     inner_width = w_out.shape[0]
-    head_dim = inner_width // HEADS
     positions = lax.axis_index("seq") * frame_count + jnp.arange(frame_count)
     frame_mask = (positions[None, :] < lengths[:, None]).astype(jnp.float32)
     counts = lengths.astype(jnp.float32) * (channels // GROUPS)
@@ -432,85 +779,45 @@
     resnet_out = act_two + project(masked_in, conv_skip) + shifts[5]
     normed_one = layer_norm(resnet_out, gains[2], shifts[6]).astype(jnp.bfloat16)
     qkv_rows = project(normed_one, w_qkv).astype(jnp.bfloat16)
-    queries = qkv_rows[:, :, :inner_width].reshape(utt_count, frame_count, HEADS, head_dim)
-    keys_all, values_all = (
-        lax.all_gather(qkv_rows[:, :, inner_width : 2 * inner_width], "seq", axis=1, tiled=True),
-        lax.all_gather(qkv_rows[:, :, 2 * inner_width :], "seq", axis=1, tiled=True),
-    )
-    attended_full, queries_aug = attn_forward(
-        lengths, qkv_rows[:, :, :inner_width], keys_all, values_all
-    )
-    attended = attended_full.astype(BF)
-    resid_two = resnet_out + project(attended, w_out) + shifts[7]
-    normed_two = layer_norm(resid_two, gains[3], shifts[8]).astype(jnp.bfloat16)
-    ff_hidden = project(normed_two, ff_in) + ff_bias
-    snaked = snake(ff_hidden, snake_logs).astype(jnp.bfloat16)
-    resid_three = resid_two + project(snaked, ff_out) + shifts[9]
-    down_in = (resid_three * column_mask).astype(jnp.bfloat16)
-    half_len = frame_count // 2
-    before_first = from_behind(down_in[:, frame_count - 1 :], "seq", 1)
-    frame_pairs = down_in.reshape(utt_count, half_len, 2, channels)
-    even_rows = frame_pairs[:, :, 0]
-    odd_rows = frame_pairs[:, :, 1]
-    before = jnp.concatenate([before_first, odd_rows[:, : half_len - 1]], axis=1)
-    taps_down = jnp.concatenate([before, even_rows, odd_rows], axis=2)
-    half_mask = frame_mask[:, 0::2][:, :, None]
-    lowered = project(taps_down, conv_down.reshape(-1, channels)) + shifts[10]
-    layer_out = (lowered * half_mask).astype(jnp.bfloat16)
-    grad_lowered = out_cotangent.astype(jnp.float32) * half_mask
-    grad_shift_down = jnp.sum(grad_lowered, axis=(0, 1))
-    grad_low = grad_lowered.astype(jnp.bfloat16)
-    grad_conv_down = weight_grad(taps_down, grad_low).reshape(3, channels, channels)
-    grad_taps = project_back(grad_low, conv_down.reshape(-1, channels))
-    grad_before = grad_taps[:, :, :channels]
-    grad_evens = grad_taps[:, :, channels : 2 * channels]
-    grad_odds = grad_taps[:, :, 2 * channels :]
-    from_next = from_behind(grad_before[:, 0:1], "seq", -1)
-    grad_odds = grad_odds + jnp.concatenate([grad_before[:, 1:], from_next], axis=1)
-    grad_down_in = jnp.stack([grad_evens, grad_odds], axis=2).reshape(
-        utt_count, frame_count, channels
-    )
-    grad_three = grad_down_in * column_mask
-    grad_shift_ff = jnp.sum(grad_three, axis=(0, 1))
-    grad_ff_low = grad_three.astype(jnp.bfloat16)
-    grad_ff_out = weight_grad(snaked, grad_ff_low)
-    grad_snaked = project_back(grad_ff_low, ff_out)
-    outputs, snake_pull = jax.vjp(snake, ff_hidden, snake_logs)
-    grad_hidden, grad_snake_logs = snake_pull(grad_snaked)
-    grad_ff_bias = jnp.sum(grad_hidden, axis=(0, 1))
-    grad_hidden_low = grad_hidden.astype(jnp.bfloat16)
-    grad_ff_in = weight_grad(normed_two, grad_hidden_low)
-    grad_normed_two = project_back(grad_hidden_low, ff_in)
-    outputs, norm_pull_two = jax.vjp(layer_norm, resid_two, gains[3], shifts[8])
-    grad_resid_norm, grad_gain_three, grad_shift_three = norm_pull_two(grad_normed_two)
-    grad_two = grad_three + grad_resid_norm
-    grad_shift_attn = jnp.sum(grad_two, axis=(0, 1))
-    grad_attn_low = grad_two.astype(jnp.bfloat16)
-    grad_w_out = weight_grad(attended, grad_attn_low)
-    grad_attended = project_back(grad_attn_low, w_out).astype(jnp.bfloat16)
-    row_terms = jnp.sum(
-        (grad_attended.astype(F32) * attended_full).reshape(utt_count, frame_count, HEADS, head_dim),
-        axis=-1,
-    )
-    pieces = split_bf16(row_terms)
-    blank = jnp.zeros((utt_count, frame_count, head_dim - 3), BF)
-    grad_aug = jnp.stack(
-        [
-            jnp.concatenate([grad_attended[:, :, :head_dim], pieces[:, :, 0], blank], axis=-1),
-            jnp.concatenate([pieces[:, :, 1], blank, grad_attended[:, :, head_dim:]], axis=-1),
-        ],
-        axis=1,
-    )
-    grad_queries, key_terms, value_terms = attn_backward(
-        lengths, queries_aug, grad_aug, keys_all, values_all
-    )
-    grad_keys, grad_values = (
-        lax.psum_scatter(key_terms, "seq", scatter_dimension=1, tiled=True),
-        lax.psum_scatter(value_terms, "seq", scatter_dimension=1, tiled=True),
-    )
-    grad_qkv = jnp.concatenate(
-        [grad_queries, grad_keys, grad_values], axis=2
-    )
+    attended_full, queries_aug, kv_all = attend(
+        lengths, qkv_rows[:, :, :inner_width], qkv_rows[:, :, inner_width:]
+    )
+    next_rows = from_behind(out_cotangent[:, 0:16], "seq", -1)
+    (
+        layer_out,
+        grad_two,
+        grad_aug,
+        last_rows,
+        grad_w_out,
+        grad_ff_in,
+        grad_ff_out,
+        grad_conv_down,
+        mid_small,
+        ff_small,
+    ) = middle(
+        lengths,
+        attended_full,
+        resnet_out,
+        out_cotangent,
+        next_rows,
+        w_out,
+        ff_in,
+        ff_out,
+        conv_down,
+        gains,
+        shifts,
+        ff_bias,
+        snake_logs,
+    )
+    before_first = from_behind(last_rows, "seq", 1)[:, 15:16]
+    half_mask = frame_mask[:, 0:1][:, :, None]
+    first_low = out_cotangent[:, 0:1].astype(F32) * half_mask
+    first_out = layer_out[:, 0:1].astype(F32) + project(before_first, conv_down[0]) * half_mask
+    layer_out = layer_out.at[:, 0:1].set(first_out.astype(BF))
+    grad_conv_down = grad_conv_down.at[0].add(weight_grad(before_first, first_low.astype(BF)))
+    grad_gain_three, grad_shift_attn, grad_shift_three, grad_shift_ff, grad_shift_down = mid_small[:5]
+    grad_ff_bias, grad_snake_logs = ff_small[0], ff_small[1:3]
+    grad_qkv = attend_back(lengths, queries_aug, grad_aug, kv_all)
     grad_w_qkv = weight_grad(normed_one, grad_qkv)
     grad_normed_one = project_back(grad_qkv, w_qkv)
     outputs, norm_pull_one = jax.vjp(layer_norm, resnet_out, gains[2], shifts[6])

time: 474 us -> 327 us (0.69)
  matrix products: 102 us -> 31.1 us
  waiting for transfers between devices: 65.7 us -> 1.1 us
  Pallas kernels: 135 us -> 174 us
  local copies, waits for them, and re-layouts: 49.5 us -> 27.2 us
  between operations: 15.7 us -> 1.91 us
  other arithmetic: 35.8 us -> 23.7 us
    dot_general x10 -> x7, matrix products: 67.9 us -> 19.1 us  [project(): lax.dot_general(operand, matrix, (((operand.ndim - 1,), (0,)), ((), ())),...]
    pallas_call x2 -> x3, Pallas kernels: 74 us -> 114 us  [the longest x1 49.9 us: attend_back(): pl.pallas_call(functools.partial(backward_kernel, KB), out_shape=jax.Shap...]
    reduce_scatter x2 -> x0, waiting for transfers between devices: 30.6 us -> none  [the longest x1 30.6 us: shards(): lax.psum_scatter(value_terms, 'seq', scatter_dimension=1, tiled=True)]
    all_gather x2 -> x0, waiting for transfers between devices: 27.1 us -> none  [the longest x1 24.8 us: shards(): lax.all_gather(qkv_rows[:, :, 2 * inner_width:], 'seq', axis=1, tiled=True)]
    dot_general x6 -> x2, matrix products: 15.8 us -> 4.2 us  [project_back(): lax.dot_general(grads, matrix, (((grads.ndim - 1,), (1,)), ((), ())), pre...]
    dot_general x8 -> x5, matrix products: 17.8 us -> 7.62 us  [weight_grad(): lax.dot_general(flat_operand, flat_grads, (((0,), (0,)), ((), ())), prefe...]
    unnamed x263 -> x125, local copies, waits for them, and re-layouts: 24.3 us -> 16 us
    reshape x2 -> x0, local copies, waits for them, and re-layouts: 6.41 us -> none  [the longest x1 4.1 us: shards(): jnp.stack([grad_evens, grad_odds], axis=2)]
  transfers between devices with their start and end apart: 14 -> 10, of which waited for: 6 -> 1; matrix products, arithmetic and copies ran while one was open for 11% -> 13% of each run, Pallas kernels for 0% -> 13%
where the time goes in v3:
time: 327 us; the launch traced here: 322 us
  Pallas kernels  174 us (53%)
  blocking collectives  35.9 us (11%)
  matrix products  31.1 us (10%)
  local copies, waits for them, and re-layouts  27.2 us (8%)
  starting transfers between devices  27 us (8%)
  other arithmetic  23.7 us (7%)
    pallas_call x1, Pallas kernels, reduce_all(): pl.pallas_call(functools.partial(reduce_kernel, axes, count, len(mats)),...  59.4 us
    pallas_call x1, Pallas kernels, attend_back(): pl.pallas_call(functools.partial(backward_kernel, KB), out_shape=jax.Shap...  49.9 us
    pallas_call x1, Pallas kernels, attend(): pl.pallas_call(forward_kernel, out_shape=(jax.ShapeDtypeStruct((U, F, 128...  41.6 us
    pallas_call x1, Pallas kernels, middle(): pl.pallas_call(functools.partial(middle_kernel, RB, FC), out_shape=(jax.S...  22.9 us
    dot_general x7, matrix products, project(): lax.dot_general(operand, matrix, (((operand.ndim - 1,), (0,)), ((), ())),...  19.1 us
    unnamed x125, local copies, waits for them, and re-layouts  16 us
    psum x2, blocking collectives, group_stats(): lax.psum(jnp.sum(centered * centered * mask_cube, axis=(1, 3)), 'seq')  14.1 us
    ppermute x4, starting transfers between devices, with_halo(): before = lax.ppermute(last, axis, up)  13.1 us
  transfers between devices with their start and end apart: 10, of which 1 were waited for; matrix products, arithmetic and copies ran while one was open for 13% of the time, Pallas kernels for 13%

profile of v3, /device:TPU:1, one launch (start us, length us, event | category | flops | bytes accessed | tf_op | source)
XLA Modules:
  0.0 321.7 jit_solution(7601001243581489573)
XLA Ops:
  3.1 4.5 %collective-permute-start = (bf16[2,1,256]{2,1,0:T(2,128)(2,1)S(1)}, bf16[2,1,256]{2,1,0:T(2,128)(2,1)S(1)}, u32[]{:S(2)}, u32[]{:S(2)}) collective-permute-start(bf16[2,1,256]{2,1,0:T(2,128)(2,1)S(1)} %get-tuple-element.124), channel_id=1, source_target_pairs={{0,1},{1,2},{2,3},{4,5},{5,6},{6,7},{8,9},{9,10},{10,11},{12,13},{... | collective-permute-start | bytes 3080 | tf_op jit(solution)/shard_map/ppermute | solution.py:37
  7.7 1.9 collective-permute-start.1
  15.2 5.6 %psum.56 = f32[2,8]{1,0:T(2,128)S(1)} all-reduce(f32[2,8]{1,0:T(2,128)S(1)} %reduce_sum.330), channel_id=1, replica_groups=mesh['dp'=8,'seq'=4] {'seq'}, use_global_device_ids=true, to_apply=%region_2.0 | all-reduce | flops 16 | bytes 128 | tf_op jit(solution)/shard_map/psum | solution.py:97
  21.6 7.3 %psum.57 = f32[2,8]{1,0:T(2,128)S(1)} all-reduce(f32[2,8]{1,0:T(2,128)S(1)} %reduce_sum.333), channel_id=1, replica_groups=mesh['dp'=8,'seq'=4] {'seq'}, use_global_device_ids=true, to_apply=%region_5.6 | all-reduce | flops 16 | bytes 128 | tf_op jit(solution)/shard_map/psum | solution.py:100
  32.0 2.6 collective-permute-start.2
  34.5 1.9 collective-permute-start.3
  40.0 3.3 %multiply_reduce_fusion.9 = (f32[2,256]{1,0:T(2,128)S(1)}, f32[2,1024,256]{2,1,0:T(8,128)S(1)}) fusion(f32[256]{0:T(256)S(1)} %bitcast.113, f32[2,1024]{1,0:T(2,128)S(1)} %get-tuple-element.143, bf16[768,256,1]{1,0,2:T(8,128)(2,1)S(1)} %bitcast.97, bf16[2,1,256]{2,1,0:T(2,128)(2,1)} %copy-done.45, bf16[2,1024,256]{2,1,0:T(8,128)(2,1)} %copy-done.15, ...), kind=kOutput, calls=%fused_computation.67 | convolution fusion | flops 822607360 | bytes 3552256 | tf_op jit(solution)/shard_map/dot_general | solution.py:54
  43.5 5.2 %psum.58 = f32[2,8]{1,0:T(2,128)S(1)} all-reduce(f32[2,8]{1,0:T(2,128)S(1)} %reduce_sum.336), channel_id=1, replica_groups=mesh['dp'=8,'seq'=4] {'seq'}, use_global_device_ids=true, to_apply=%region_8.9 | all-reduce | flops 16 | bytes 128 | tf_op jit(solution)/shard_map/psum | solution.py:97
  49.5 6.9 %psum.59 = f32[2,8]{1,0:T(2,128)S(1)} all-reduce(f32[2,8]{1,0:T(2,128)S(1)} %reduce_sum.339), channel_id=1, replica_groups=mesh['dp'=8,'seq'=4] {'seq'}, use_global_device_ids=true, to_apply=%region_11.12 | all-reduce | flops 16 | bytes 128 | tf_op jit(solution)/shard_map/psum | solution.py:100
  56.6 3.4 %fusion.94 = (f32[2,1024]{1,0:T(2,128)S(1)}, f32[2,1024,256]{2,1,0:T(8,128)S(1)}) fusion(f32[256]{0:T(256)S(1)} %bitcast.138, bf16[2,1024,256]{2,1,0:T(8,128)(2,1)} %copy-done.8, bf16[256,256]{1,0:T(8,128)(2,1)S(1)} %copy-done.29, f32[2,1024]{1,0:T(2,128)S(1)} %get-tuple-element.143, f32[256]{0:T(256)S(1)} %bitcast.126, f32[256]{0:T(256)S(1)} %bitcast.121, ...), kind=kOutput, calls=%fused_computation.177 | convolution fusion | flops 276822016 | bytes 5398528 | tf_op jit(solution)/shard_map/dot_general | solution.py:54
  64.0 41.6 %attend.1 = (f32[2,1024,128]{2,1,0:T(8,128)}, bf16[2,2,1024,128]{3,2,1,0:T(8,128)(2,1)}, bf16[4,2,1024,256]{3,2,1,0:T(8,128)(2,1)}) custom-call(s32[2]{0:T(128)} %len_ref.5, bf16[2,1024,128]{2,1,0:T(8,128)(2,1)} %slice.235.q_ref, bf16[2,1024,256]{2,1,0:T(8,128)(2,1)} %slice.236.kv_ref), custom_call_target="tpu_custom_call" | custom-call | tf_op jit(solution)/shard_map/attend/pallas_call | solution.py:619
  106.2 22.9 %middle.1 = (bf16[2,512,256]{2,1,0:T(8,128)(2,1)}, f32[2,1024,256]{2,1,0:T(8,128)}, bf16[2,2,1024,128]{3,2,1,0:T(8,128)(2,1)}, bf16[2,16,256]{2,1,0:T(8,128)(2,1...) custom-call(s32[2]{0:T(128)} %len_ref.5, ...), custom_call_target="tpu_custom_call" | custom-call | tf_op jit(solution)/shard_map/middle/pallas_call | solution.py:323
  129.2 49.9 %attend_back.1 = bf16[2,1024,384]{2,1,0:T(8,128)(2,1)} custom-call(s32[2]{0:T(128)} %len_ref.5, bf16[2,2,1024,128]{3,2,1,0:T(8,128)(2,1)} %get-tuple-element.70.qa_ref, bf16[2,2,1024,128]{3,2,1,0:T(8,128)(2,1)} %get-tuple-element.71.da_ref, bf16[4,2,1024,256]{3,2,1,0:T(8,128)(2,1)} %get-tuple-element.72.all_ref), custom_call_target="tpu_custom_call" | custom-call | tf_op jit(solution)/shard_map/attend_back/pallas_call | solution.py:723
  179.1 2.4 fusion.80
  181.5 2.3 convolution_bitcast_fusion.2.refs_4_
  187.0 4.4 %multiply_reduce_fusion.1 = (f32[256]{0:T(256)S(1)}, f32[2,256]{1,0:T(2,128)S(1)}, f32[2,256]{1,0:T(2,128)S(1)}, f32[256]{0:T(256)S(1)}, f32[2,1024,256]{2,1,0:T(8,128)}) fusion(f32[2,256]{1,0:T(2,128)S(1)} %mul.430, f32[2,256]{1,0:T(2,128)S(1)} %sub.40, f32[2,1024,256]{2,1,0:T(8,128)S(1)} %copy-done.4, f32[256]{0:T(256)S(1)} %bitcast.116, ...), kind=kLoop, calls=%fused_computation.41 | loop fusion | flops 17299968 | bytes 6312960 | tf_op jit(solution)/shard_map/transpose(jvp())/reduce_sum | solution.py:111
  192.9 5.8 %all-reduce.1 = (f32[2,8]{1,0:T(2,128)S(1)}, f32[2,8]{1,0:T(2,128)S(1)}) all-reduce(f32[2,8]{1,0:T(2,128)S(1)} %reduce_sum.349, f32[2,8]{1,0:T(2,128)S(1)} %neg.27), channel_id=1, replica_groups=mesh['dp'=8,'seq'=4] {'seq'}, use_global_device_ids=true, to_apply=%region_21.23 | all-reduce | flops 32 | bytes 256 | tf_op jit(solution)/shard_map/psum | solution.py:121
  199.2 3.1 fusion.82
  202.2 2.7 collective-permute-start.6
  204.9 2.9 collective-permute-start.7
  207.9 2.4 collective-permute-start.5
  210.3 1.9 convolution_bitcast_fusion.refs_1_
  213.1 5.9 %multiply_reduce_fusion.2 = (f32[256]{0:T(256)S(1)}, f32[2,256]{1,0:T(2,128)S(1)}, f32[2,256]{1,0:T(2,128)S(1)}, f32[256]{0:T(256)S(1)}, f32[2,1024,256]{2,1,0:T...) fusion(f32[2,256]{1,0:T(2,128)S(1)} %mul.416, f32[2,256]{1,0:T(2,128)S(1)} %sub.36, f32[2,1024,256]{2,1,0:T(8,128)S(1)} %copy-done.6, ...), kind=kOutput, calls=%fused_computation.42 | convolution fusion | flops 839383296 | bytes 7757824 | tf_op jit(solution)/shard_map/dot_general | solution.py:54
  219.4 5.2 %all-reduce = (f32[2,8]{1,0:T(2,128)S(1)}, f32[2,8]{1,0:T(2,128)S(1)}) all-reduce(f32[2,8]{1,0:T(2,128)S(1)} %reduce_sum.355, f32[2,8]{1,0:T(2,128)S(1)} %neg.28), channel_id=1, replica_groups=mesh['dp'=8,'seq'=4] {'seq'}, use_global_device_ids=true, to_apply=%region_27.29 | all-reduce | flops 32 | bytes 256 | tf_op jit(solution)/shard_map/psum | solution.py:121
  224.9 3.1 fusion.83
  228.1 3.0 collective-permute-start.8
  231.1 3.2 collective-permute-start.9
  234.6 2.0 multiply_reduce_fusion.3.refs_3_
  236.6 1.9 convolution_bitcast_fusion.1.refs_0_
  239.1 3.1 fusion.2
  245.3 59.4 %reduce_weights.1 = (f32[768,256]{1,0:T(8,128)}, f32[768,256]{1,0:T(8,128)}, f32[256,256]{1,0:T(8,128)}, f32[1024,256]{1,0:T(8,128)}, f32[256,384]{1,0:T(8,128)}...) custom-call(f32[768,256]{1,0:T(8,128)} %convolution_bitcast_fusion.1, ...), custom_call_target="tpu_custom_call" | custom-call | tf_op jit(solution)/shard_map/reduce_weights/pallas_call | solution.py:475
  312.6 2.1 copy.115
  (219 shorter events, 46.2 us)
Async XLA Ops:
  0.6 12.6 %copy-start = (bf16[1024,256]{1,0:T(8,128)(2,1)S(1)}, bf16[1024,256]{1,0:T(8,128)(2,1)}, u32[]{:S(2)}) copy-start(bf16[1024,256]{1,0:T(8,128)(2,1)} %param.29) | copy-start | bytes 1572868
  0.7 11.6 %copy-start.34 = (s32[2]{0:T(128)S(1)}, s32[2]{0:T(128)}, u32[]{:S(2)}) copy-start(s32[2]{0:T(128)} %len_ref.5) | copy-start | bytes 28
  0.7 12.6 %copy-start.33 = (f32[4,256]{1,0:T(4,128)S(1)}, f32[4,256]{1,0:T(4,128)}, u32[]{:S(2)}) copy-start(f32[4,256]{1,0:T(4,128)} %gains.1) | copy-start | bytes 12292
  0.7 12.6 %copy-start.32 = (bf16[2,1024]{1,0:T(2,128)(2,1)S(1)}, bf16[2,1024]{1,0:T(2,128)(2,1)}, u32[]{:S(2)}) copy-start(bf16[2,1024]{1,0:T(2,128)(2,1)} %param.23) | copy-start | bytes 12292
  0.7 13.0 %copy-start.24 = (bf16[3,256,256]{2,1,0:T(8,128)(2,1)S(1)}, bf16[3,256,256]{2,1,0:T(8,128)(2,1)}, u32[]{:S(2)}) copy-start(bf16[3,256,256]{2,1,0:T(8,128)(2,1)} %param.26) | copy-start | bytes 1179652
  3.1 11.9 %copy-start.8 = (bf16[2,1024,256]{2,1,0:T(8,128)(2,1)}, bf16[2,1024,256]{2,1,0:T(8,128)(2,1)S(1)}, u32[]{:S(2)}) copy-start(bf16[2,1024,256]{2,1,0:T(8,128)(2,1)S(1)} %broadcast_multiply_fusion) | copy-start | bytes 3145732
  3.1 10.5 %collective-permute-start = (bf16[2,1,256]{2,1,0:T(2,128)(2,1)S(1)}, bf16[2,1,256]{2,1,0:T(2,128)(2,1)S(1)}, u32[]{:S(2)}, u32[]{:S(2)}) collective-permute-start(bf16[2,1,256]{2,1,0:T(2,128)(2,1)S(1)} %get-tuple-element.124), channel_id=1, source_target_pairs={{0,1},{1,2},{2,3},{4,5},{5,6},{6,7},{8,9},{9,10},{10,11},{12,13},{... | collective-permute-start | bytes 3080 | tf_op jit(solution)/shard_map/ppermute | solution.py:37
  7.7 6.0 %collective-permute-start.1 = (bf16[2,1,256]{2,1,0:T(2,128)(2,1)S(1)}, bf16[2,1,256]{2,1,0:T(2,128)(2,1)S(1)}, u32[]{:S(2)}, u32[]{:S(2)}) collective-permute-start(bf16[2,1,256]{2,1,0:T(2,128)(2,1)S(1)} %get-tuple-element.125), channel_id=1, source_target_pairs={{1,0},{2,1},{3,2},{5,4},{6,5},{7,6},{9,8},{10,9},{11,10},{13,12},{... | collective-permute-start | bytes 3080 | tf_op jit(solution)/shard_map/ppermute | solution.py:38
  10.3 95.3 %collective-permute-start.4 = (bf16[2,16,256]{2,1,0:T(8,128)(2,1)S(1)}, bf16[2,16,256]{2,1,0:T(8,128)(2,1)S(1)}, u32[]{:S(2)}, u32[]{:S(2)}) collective-permute-start(bf16[2,16,256]{2,1,0:T(8,128)(2,1)S(1)} %slice.210), channel_id=1, source_target_pairs={{1,0},{2,1},{3,2},{5,4},{6,5},{7,6},{9,8},{10,9},{11,10},{13,12},{... | collective-permute-start | bytes 49160 | tf_op jit(solution)/shard_map/ppermute | solution.py:46
  13.6 22.9 %copy-start.36 = (f32[2]{0:T(128)}, f32[2]{0:T(128)S(1)}, u32[]{:S(2)}) copy-start(f32[2]{0:T(128)S(1)} %slice_reduce_fusion) | copy-start | bytes 28
  15.1 15.9 %copy-start.5 = (f32[2,1024,256]{2,1,0:T(8,128)}, f32[2,1024,256]{2,1,0:T(8,128)S(1)}, u32[]{:S(2)}) copy-start(f32[2,1024,256]{2,1,0:T(8,128)S(1)} %get-tuple-element.149) | copy-start | bytes 6291460
  21.4 16.7 %copy-start.25 = (bf16[3,256,256]{2,1,0:T(8,128)(2,1)S(1)}, bf16[3,256,256]{2,1,0:T(8,128)(2,1)}, u32[]{:S(2)}) copy-start(bf16[3,256,256]{2,1,0:T(8,128)(2,1)} %param.27) | copy-start | bytes 1179652
  32.0 6.4 %collective-permute-start.2 = (bf16[2,1,256]{2,1,0:T(2,128)(2,1)S(1)}, bf16[2,1,256]{2,1,0:T(2,128)(2,1)S(1)}, u32[]{:S(2)}, u32[]{:S(2)}) collective-permute-start(bf16[2,1,256]{2,1,0:T(2,128)(2,1)S(1)} %get-tuple-element.122), channel_id=1, source_target_pairs={{0,1},{1,2},{2,3},{4,5},{5,6},{6,7},{8,9},{9,10},{10,11},{12,13},{... | collective-permute-start | bytes 3080 | tf_op jit(solution)/shard_map/ppermute | solution.py:37
  34.5 4.9 %collective-permute-start.3 = (bf16[2,1,256]{2,1,0:T(2,128)(2,1)S(1)}, bf16[2,1,256]{2,1,0:T(2,128)(2,1)S(1)}, u32[]{:S(2)}, u32[]{:S(2)}) collective-permute-start(bf16[2,1,256]{2,1,0:T(2,128)(2,1)S(1)} %get-tuple-element.123), channel_id=1, source_target_pairs={{1,0},{2,1},{3,2},{5,4},{6,5},{7,6},{9,8},{10,9},{11,10},{13,12},{... | collective-permute-start | bytes 3080 | tf_op jit(solution)/shard_map/ppermute | solution.py:38
  43.3 16.7 %copy-start.3 = (f32[2,1024,256]{2,1,0:T(8,128)}, f32[2,1024,256]{2,1,0:T(8,128)S(1)}, u32[]{:S(2)}) copy-start(f32[2,1024,256]{2,1,0:T(8,128)S(1)} %get-tuple-element.151) | copy-start | bytes 6291460
  43.3 13.3 %copy-start.29 = (bf16[256,256]{1,0:T(8,128)(2,1)S(1)}, bf16[256,256]{1,0:T(8,128)(2,1)}, u32[]{:S(2)}) copy-start(bf16[256,256]{1,0:T(8,128)(2,1)} %param.28) | copy-start | bytes 393220
  129.2 49.9 %copy-start.2 = (f32[2,1024,256]{2,1,0:T(8,128)S(1)}, f32[2,1024,256]{2,1,0:T(8,128)}, u32[]{:S(2)}) copy-start(f32[2,1024,256]{2,1,0:T(8,128)} %copy-done.1) | copy-start | bytes 6291460
  199.1 8.7 %copy-start.38 = (bf16[2,16,256]{2,1,0:T(8,128)(2,1)S(1)}, bf16[2,16,256]{2,1,0:T(8,128)(2,1)}, u32[]{:S(2)}) copy-start(bf16[2,16,256]{2,1,0:T(8,128)(2,1)} %get-tuple-element.68) | copy-start | bytes 49156
  199.1 11.1 %copy-start.16 = (bf16[2,1024,256]{2,1,0:T(8,128)(2,1)S(1)}, bf16[2,1024,256]{2,1,0:T(8,128)(2,1)}, u32[]{:S(2)}) copy-start(bf16[2,1024,256]{2,1,0:T(8,128)(2,1)} %copy-done.15) | copy-start | bytes 3145732
  199.1 11.1 %copy-start.44 = (bf16[2,1,256]{2,1,0:T(2,128)(2,1)S(1)}, bf16[2,1,256]{2,1,0:T(2,128)(2,1)}, u32[]{:S(2)}) copy-start(bf16[2,1,256]{2,1,0:T(2,128)(2,1)} %copy-done.43) | copy-start | bytes 3076
  199.1 11.1 %copy-start.46 = (bf16[2,1,256]{2,1,0:T(2,128)(2,1)S(1)}, bf16[2,1,256]{2,1,0:T(2,128)(2,1)}, u32[]{:S(2)}) copy-start(bf16[2,1,256]{2,1,0:T(2,128)(2,1)} %copy-done.45) | copy-start | bytes 3076
  202.2 10.8 %collective-permute-start.6 = (bf16[2,1,256]{2,1,0:T(2,128)(2,1)S(1)}, bf16[2,1,256]{2,1,0:T(2,128)(2,1)S(1)}, u32[]{:S(2)}, u32[]{:S(2)}) collective-permute-start(bf16[2,1,256]{2,1,0:T(2,128)(2,1)S(1)} %get-tuple-element.120), channel_id=1, source_target_pairs={{1,0},{2,1},{3,2},{5,4},{6,5},{7,6},{9,8},{10,9},{11,10},{13,12},{... | collective-permute-start | bytes 3080 | tf_op jit(solution)/shard_map/ppermute | solution.py:38
  204.9 8.2 %collective-permute-start.7 = (bf16[2,1,256]{2,1,0:T(2,128)(2,1)S(1)}, bf16[2,1,256]{2,1,0:T(2,128)(2,1)S(1)}, u32[]{:S(2)}, u32[]{:S(2)}) collective-permute-start(bf16[2,1,256]{2,1,0:T(2,128)(2,1)S(1)} %get-tuple-element.121), channel_id=1, source_target_pairs={{0,1},{1,2},{2,3},{4,5},{5,6},{6,7},{8,9},{9,10},{10,11},{12,13},{... | collective-permute-start | bytes 3080 | tf_op jit(solution)/shard_map/ppermute | solution.py:37
  207.9 36.3 %collective-permute-start.5 = (bf16[2,16,256]{2,1,0:T(8,128)(2,1)S(1)}, bf16[2,16,256]{2,1,0:T(8,128)(2,1)S(1)}, u32[]{:S(2)}, u32[]{:S(2)}) collective-permute-start(bf16[2,16,256]{2,1,0:T(8,128)(2,1)S(1)} %copy-done.38), channel_id=1, source_target_pairs={{0,1},{1,2},{2,3},{4,5},{5,6},{6,7},{8,9},{9,10},{10,11},{12,13},{... | collective-permute-start | bytes 49160 | tf_op jit(solution)/shard_map/ppermute | solution.py:46
  224.9 9.6 %copy-start.12 = (f32[2,1024,256]{2,1,0:T(8,128)S(1)}, f32[2,1024,256]{2,1,0:T(8,128)}, u32[]{:S(2)}) copy-start(f32[2,1024,256]{2,1,0:T(8,128)} %get-tuple-element.155) | copy-start | bytes 6291460
  228.1 10.4 %copy-start.17 = (bf16[2,1024,256]{2,1,0:T(8,128)(2,1)}, bf16[2,1024,256]{2,1,0:T(8,128)(2,1)S(1)}, u32[]{:S(2)}) copy-start(bf16[2,1024,256]{2,1,0:T(8,128)(2,1)S(1)} %get-tuple-element.114) | copy-start | bytes 3145732
  228.1 11.0 %collective-permute-start.8 = (bf16[2,1,256]{2,1,0:T(2,128)(2,1)S(1)}, bf16[2,1,256]{2,1,0:T(2,128)(2,1)S(1)}, u32[]{:S(2)}, u32[]{:S(2)}) collective-permute-start(bf16[2,1,256]{2,1,0:T(2,128)(2,1)S(1)} %get-tuple-element.118), channel_id=1, source_target_pairs={{1,0},{2,1},{3,2},{5,4},{6,5},{7,6},{9,8},{10,9},{11,10},{13,12},{... | collective-permute-start | bytes 3080 | tf_op jit(solution)/shard_map/ppermute | solution.py:38
  231.1 8.0 %collective-permute-start.9 = (bf16[2,1,256]{2,1,0:T(2,128)(2,1)S(1)}, bf16[2,1,256]{2,1,0:T(2,128)(2,1)S(1)}, u32[]{:S(2)}, u32[]{:S(2)}) collective-permute-start(bf16[2,1,256]{2,1,0:T(2,128)(2,1)S(1)} %get-tuple-element.119), channel_id=1, source_target_pairs={{0,1},{1,2},{2,3},{4,5},{5,6},{6,7},{8,9},{9,10},{10,11},{12,13},{... | collective-permute-start | bytes 3080 | tf_op jit(solution)/shard_map/ppermute | solution.py:37
  245.3 63.0 %copy-start.37 = (f32[2]{0:T(128)S(1)}, f32[2]{0:T(128)}, u32[]{:S(2)}) copy-start(f32[2]{0:T(128)} %copy-done.36) | copy-start | bytes 28
  304.7 9.9 %copy-start.23 = (f32[768,256]{1,0:T(8,128)S(1)}, f32[768,256]{1,0:T(8,128)}, u32[]{:S(2)}) copy-start(f32[768,256]{1,0:T(8,128)} %get-tuple-element.84) | copy-start | bytes 2359300
  304.8 10.8 %copy-start.28 = (f32[256,256]{1,0:T(8,128)S(1)}, f32[256,256]{1,0:T(8,128)}, u32[]{:S(2)}) copy-start(f32[256,256]{1,0:T(8,128)} %get-tuple-element.179) | copy-start | bytes 786436
  304.8 11.5 %copy-start.20 = (f32[1024,256]{1,0:T(8,128)S(1)}, f32[1024,256]{1,0:T(8,128)}, u32[]{:S(2)}) copy-start(f32[1024,256]{1,0:T(8,128)} %get-tuple-element.180) | copy-start | bytes 3145732
  (25 other events, 78.3 us)
